TPU v7x, 32 devices: a whole 2x2x4 slice. The times are simulated.
32 devices in a mesh: dp: 8 (over z, x), fsdp: 4 (over y, core).
Axes of the slice: x: 2, y: 2, z: 4, core: 2. Of those that a mesh axis runs over, the one named last changes fastest.
Arguments:
- tokens: bfloat16 [5120, 768], P(('dp', 'fsdp')), may hold values from -6 to 6
- image_tokens: bfloat16 [128, 256, 768], P(('dp', 'fsdp')), may hold values from -6 to 6
- caption_lengths: int32 [32, 4], P(('dp', 'fsdp')), may hold values from 1 to 64, 160 in all within a row
- arrival_order: int32 [32, 160], P(('dp', 'fsdp')), may hold values from 0 to 159, each once within a row
- w_qkv: bfloat16 [1769472], P(('dp', 'fsdp')), may hold values from -0.21875 to 0.21875
- w_out: bfloat16 [589824], P(('dp', 'fsdp')), may hold values from -0.4375 to 0.4375
- w_cross_q: bfloat16 [589824], P(('dp', 'fsdp')), may hold values from -0.21875 to 0.21875
- w_cross_kv: bfloat16 [1179648], P(('dp', 'fsdp')), may hold values from -0.21875 to 0.21875
- w_cross_out: bfloat16 [589824], P(('dp', 'fsdp')), may hold values from -0.875 to 0.875
- w_up: bfloat16 [2359296], P(('dp', 'fsdp')), may hold values from -0.21875 to 0.21875
- w_down: bfloat16 [2359296], P(('dp', 'fsdp')), may hold values from -0.109375 to 0.109375
- small_params: bfloat16 [8448], P(('dp', 'fsdp')), may hold values from -0.5 to 1.5
- cotangent: bfloat16 [5120, 768], P(('dp', 'fsdp')), may hold values from -6 to 6
Outputs:
- layer_out: bfloat16 [5120, 768], P(('dp', 'fsdp'))
- grad_tokens: bfloat16 [5120, 768], P(('dp', 'fsdp'))
- grad_image: bfloat16 [128, 256, 768], P(('dp', 'fsdp'))
- grad_qkv: float32 [1769472], P(('dp', 'fsdp'))
- grad_out: float32 [589824], P(('dp', 'fsdp'))
- grad_cross_q: float32 [589824], P(('dp', 'fsdp'))
- grad_cross_kv: float32 [1179648], P(('dp', 'fsdp'))
- grad_cross_out: float32 [589824], P(('dp', 'fsdp'))
- grad_up: float32 [2359296], P(('dp', 'fsdp'))
- grad_down: float32 [2359296], P(('dp', 'fsdp'))
- grad_small: float32 [8448], P(('dp', 'fsdp'))
All inputs are finite; a program needn't handle non-finite values.
Results may differ from a plain program's by a relative error of at most 0.018.
Values may be sent and summed in bfloat16 or wider, within the bound.
No kernel may reach another device: no remote copies, remote signals or barrier semaphores. Data moves between devices by JAX's collectives and lax.ppermute only.
A program may use at most 128 MiB of HBM per device.

v0:
```python
import jax
import jax.numpy as jnp
from jax import lax
from jax.sharding import PartitionSpec as P

D = 768
HEAD_DIM = 64
FF = 3072
V = 768
IMG = 256
CAP_LEN = 64


epsilon = 1e-05
masked_fill = 1e30


def norm_rows(inputs, gain_vec, shift_vec):
    centred = inputs - jnp.mean(inputs, axis=-1, keepdims=True)
    variance = jnp.mean(centred * centred, axis=-1, keepdims=True)
    return centred * lax.rsqrt(variance + epsilon) * gain_vec + shift_vec


def norm_back(inputs, gain_vec, shift_vec, grad_normed):
    _, pullback = jax.vjp(norm_rows, inputs, gain_vec, shift_vec)
    return pullback(grad_normed)


def gelu_exact(inputs):
    return jax.nn.gelu(inputs, approximate=False)


def gelu_back(inputs, grad_active):
    _, pullback = jax.vjp(gelu_exact, inputs)
    return pullback(grad_active)[0]


def slot_index(lengths, arrivals):
    run_ends = jnp.cumsum(lengths)
    starts = run_ends - lengths
    caption = jnp.sum((run_ends[None, :] <= arrivals[:, None]).astype(jnp.int32), axis=1)
    picked = caption[:, None] == jnp.arange(lengths.shape[0], dtype=jnp.int32)[None, :]
    first_row = jnp.sum(jnp.where(picked, starts[None, :], 0), axis=1)
    return caption * CAP_LEN + arrivals - first_row


def score_block(queries, keys_in, allowed):
    scores = jnp.einsum(
        "cqhd,ckhd->chqk", queries, keys_in, preferred_element_type=jnp.float32
    ) * HEAD_DIM ** (-0.5)
    return jnp.where(allowed, scores, -masked_fill)


def attention(queries, keys_in, values, allowed):
    scores = score_block(queries, keys_in, allowed)
    row_max = jnp.max(scores, axis=-1, keepdims=True)
    log_total = row_max + jnp.log(jnp.sum(jnp.exp(scores - row_max), axis=-1, keepdims=True))
    attn_weights = jnp.exp(scores - log_total).astype(jnp.bfloat16)
    mixed_out = jnp.einsum(
        "chqk,ckhd->cqhd", attn_weights, values, preferred_element_type=jnp.float32
    ).astype(jnp.bfloat16)
    return (mixed_out, log_total)


def attention_back(queries, keys_in, values, log_total, grad_mixed, allowed):
    scores = score_block(queries, keys_in, allowed)
    attn_weights = jnp.exp(scores - log_total)
    grad_weights = jnp.einsum(
        "cqhd,ckhd->chqk", grad_mixed, values, preferred_element_type=jnp.float32
    )
    centre = jnp.sum(attn_weights * grad_weights, axis=-1, keepdims=True)
    grad_scores = (attn_weights * (grad_weights - centre)).astype(jnp.bfloat16)
    grad_queries = jnp.einsum(
        "chqk,ckhd->cqhd", grad_scores, keys_in, preferred_element_type=jnp.float32
    ) * HEAD_DIM ** (-0.5)
    grad_keys = jnp.einsum(
        "chqk,cqhd->ckhd", grad_scores, queries, preferred_element_type=jnp.float32
    ) * HEAD_DIM ** (-0.5)
    grad_values = jnp.einsum(
        "chqk,cqhd->ckhd",
        attn_weights.astype(jnp.bfloat16),
        grad_mixed,
        preferred_element_type=jnp.float32,
    )
    return (grad_queries, grad_keys, grad_values)


def unpack_params(gathered):
    (
        flat_qkv,
        flat_out,
        flat_cross_q,
        flat_cross_kv,
        flat_cross_out,
        flat_up,
        flat_down,
        flat_small,
    ) = gathered
    small_vals = flat_small.astype(jnp.float32)
    return (
        flat_qkv.reshape(D, 3 * D),
        flat_out.reshape(D, D),
        flat_cross_q.reshape(D, D),
        flat_cross_kv.reshape(V, 2 * D),
        flat_cross_out.reshape(D, D),
        flat_up.reshape(D, FF),
        flat_down.reshape(FF, D),
        small_vals[: 3 * D].reshape(3, D),
        small_vals[3 * D : 6 * D].reshape(3, D),
        small_vals[6 * D : 6 * D + FF],
        small_vals[6 * D + FF :],
    )


def forward(slotted, image_rows, params, allowed, open_mask):
    (
        mat_qkv,
        mat_out,
        mat_cross_q,
        mat_cross_kv,
        mat_cross_out,
        mat_up,
        mat_down,
        norm_gains,
        shifts,
        up_bias,
        down_bias,
    ) = params
    captions = slotted.shape[0] // CAP_LEN
    head_count = D // HEAD_DIM
    normed_self = norm_rows(slotted, norm_gains[0], shifts[0]).astype(jnp.bfloat16)
    projected = jnp.dot(normed_self, mat_qkv, preferred_element_type=jnp.float32).astype(
        jnp.bfloat16
    )
    projected = projected.reshape(captions, CAP_LEN, 3, head_count, HEAD_DIM)
    self_mixed, self_total = attention(
        projected[:, :, 0], projected[:, :, 1], projected[:, :, 2], allowed
    )
    self_mixed = self_mixed.reshape(-1, D)
    after_self = slotted + jnp.dot(self_mixed, mat_out, preferred_element_type=jnp.float32)
    normed_cross = norm_rows(after_self, norm_gains[1], shifts[1]).astype(jnp.bfloat16)
    cross_query = jnp.dot(normed_cross, mat_cross_q, preferred_element_type=jnp.float32).astype(
        jnp.bfloat16
    )
    cross_query = cross_query.reshape(captions, CAP_LEN, head_count, HEAD_DIM)
    image_kv = jnp.dot(image_rows, mat_cross_kv, preferred_element_type=jnp.float32).astype(
        jnp.bfloat16
    )
    image_kv = image_kv.reshape(captions, IMG, 2, head_count, HEAD_DIM)
    cross_mixed, cross_total = attention(
        cross_query, image_kv[:, :, 0], image_kv[:, :, 1], open_mask
    )
    cross_mixed = cross_mixed.reshape(-1, D)
    after_cross = after_self + jnp.dot(
        cross_mixed, mat_cross_out, preferred_element_type=jnp.float32
    )
    normed_mlp = norm_rows(after_cross, norm_gains[2], shifts[2]).astype(jnp.bfloat16)
    hidden = jnp.dot(normed_mlp, mat_up, preferred_element_type=jnp.float32) + up_bias
    activated = gelu_exact(hidden).astype(jnp.bfloat16)
    result = (
        after_cross + jnp.dot(activated, mat_down, preferred_element_type=jnp.float32) + down_bias
    )
    saved_state = (
        slotted,
        normed_self,
        projected,
        self_total,
        self_mixed,
        after_self,
        normed_cross,
        cross_query,
        image_kv,
        cross_total,
        cross_mixed,
        after_cross,
        normed_mlp,
        hidden,
        activated,
    )
    return (result, saved_state)


def backward(saved_state, grad_slot, image_rows, params, allowed, open_mask):
    (
        mat_qkv,
        mat_out,
        mat_cross_q,
        mat_cross_kv,
        mat_cross_out,
        mat_up,
        mat_down,
        norm_gains,
        shifts,
        up_bias,
        down_bias,
    ) = params
    (
        slotted,
        normed_self,
        projected,
        self_total,
        self_mixed,
        after_self,
        normed_cross,
        cross_query,
        image_kv,
        cross_total,
        cross_mixed,
        after_cross,
        normed_mlp,
        hidden,
        activated,
    ) = saved_state
    captions = slotted.shape[0] // CAP_LEN
    head_count = D // HEAD_DIM
    grad_branch = grad_slot.astype(jnp.bfloat16)
    grad_down = jnp.einsum("rf,rd->fd", activated, grad_branch, preferred_element_type=jnp.float32)
    grad_down_bias = jnp.sum(grad_slot, axis=0)
    grad_active = jnp.einsum("rd,fd->rf", grad_branch, mat_down, preferred_element_type=jnp.float32)
    grad_hidden = gelu_back(hidden, grad_active).astype(jnp.bfloat16)
    grad_up = jnp.einsum("rd,rf->df", normed_mlp, grad_hidden, preferred_element_type=jnp.float32)
    grad_up_bias = jnp.sum(grad_hidden.astype(jnp.float32), axis=0)
    grad_normed = jnp.einsum("rf,df->rd", grad_hidden, mat_up, preferred_element_type=jnp.float32)
    grad_cross_in, grad_gain3, grad_shift3 = norm_back(
        after_cross, norm_gains[2], shifts[2], grad_normed
    )
    grad_after_cross = grad_slot + grad_cross_in
    grad_branch = grad_after_cross.astype(jnp.bfloat16)
    grad_cross_out = jnp.einsum(
        "rd,re->de", cross_mixed, grad_branch, preferred_element_type=jnp.float32
    )
    grad_mixed = jnp.einsum(
        "re,de->rd", grad_branch, mat_cross_out, preferred_element_type=jnp.float32
    ).astype(jnp.bfloat16)
    grad_mixed = grad_mixed.reshape(captions, CAP_LEN, head_count, HEAD_DIM)
    grad_query, grad_key, grad_value = attention_back(
        cross_query, image_kv[:, :, 0], image_kv[:, :, 1], cross_total, grad_mixed, open_mask
    )
    grad_query = grad_query.reshape(-1, D).astype(jnp.bfloat16)
    grad_kv = jnp.stack([grad_key, grad_value], axis=2).reshape(-1, 2 * D).astype(jnp.bfloat16)
    grad_cross_q = jnp.einsum(
        "rd,re->de", normed_cross, grad_query, preferred_element_type=jnp.float32
    )
    grad_cross_kv = jnp.einsum("iv,ie->ve", image_rows, grad_kv, preferred_element_type=jnp.float32)
    grad_image = jnp.einsum(
        "ie,ve->iv", grad_kv, mat_cross_kv, preferred_element_type=jnp.float32
    ).astype(jnp.bfloat16)
    grad_normed = jnp.einsum(
        "re,de->rd", grad_query, mat_cross_q, preferred_element_type=jnp.float32
    )
    grad_self_in, grad_gain2, grad_shift2 = norm_back(
        after_self, norm_gains[1], shifts[1], grad_normed
    )
    grad_after_self = grad_after_cross + grad_self_in
    grad_branch = grad_after_self.astype(jnp.bfloat16)
    grad_out = jnp.einsum("rd,re->de", self_mixed, grad_branch, preferred_element_type=jnp.float32)
    grad_mixed = jnp.einsum(
        "re,de->rd", grad_branch, mat_out, preferred_element_type=jnp.float32
    ).astype(jnp.bfloat16)
    grad_mixed = grad_mixed.reshape(captions, CAP_LEN, head_count, HEAD_DIM)
    grad_query, grad_key, grad_value = attention_back(
        projected[:, :, 0], projected[:, :, 1], projected[:, :, 2], self_total, grad_mixed, allowed
    )
    grad_projected = (
        jnp.stack([grad_query, grad_key, grad_value], axis=2)
        .reshape(-1, 3 * D)
        .astype(jnp.bfloat16)
    )
    grad_w_qkv = jnp.einsum(
        "rd,re->de", normed_self, grad_projected, preferred_element_type=jnp.float32
    )
    grad_normed = jnp.einsum(
        "re,de->rd", grad_projected, mat_qkv, preferred_element_type=jnp.float32
    )
    grad_input, grad_gain1, grad_shift1 = norm_back(slotted, norm_gains[0], shifts[0], grad_normed)
    grad_input = grad_input + grad_after_self
    grad_small = jnp.concatenate(
        [
            grad_gain1,
            grad_gain2,
            grad_gain3,
            grad_shift1,
            grad_shift2,
            grad_shift3,
            grad_up_bias,
            grad_down_bias,
        ]
    )
    flat_grads = (
        grad_w_qkv.reshape(-1),
        grad_out.reshape(-1),
        grad_cross_q.reshape(-1),
        grad_cross_kv.reshape(-1),
        grad_cross_out.reshape(-1),
        grad_up.reshape(-1),
        grad_down.reshape(-1),
        grad_small,
    )
    return (grad_input, grad_image, flat_grads)


def sum_to_owners(flat_grads):
    inner_count = lax.axis_size("dp")
    outer_count = lax.axis_size("fsdp")
    blocks = tuple((grad_vec.reshape(inner_count, outer_count, -1) for grad_vec in flat_grads))
    p0, p1, p2, p3, p4, p5, p6, p7 = blocks
    received = (
        lax.all_to_all(
            p0.astype(jnp.bfloat16), "dp", split_axis=0, concat_axis=0, tiled=True
        ).astype(p0.dtype),
        lax.all_to_all(
            p1.astype(jnp.bfloat16), "dp", split_axis=0, concat_axis=0, tiled=True
        ).astype(p1.dtype),
        lax.all_to_all(
            p2.astype(jnp.bfloat16), "dp", split_axis=0, concat_axis=0, tiled=True
        ).astype(p2.dtype),
        lax.all_to_all(
            p3.astype(jnp.bfloat16), "dp", split_axis=0, concat_axis=0, tiled=True
        ).astype(p3.dtype),
        lax.all_to_all(
            p4.astype(jnp.bfloat16), "dp", split_axis=0, concat_axis=0, tiled=True
        ).astype(p4.dtype),
        lax.all_to_all(
            p5.astype(jnp.bfloat16), "dp", split_axis=0, concat_axis=0, tiled=True
        ).astype(p5.dtype),
        lax.all_to_all(
            p6.astype(jnp.bfloat16), "dp", split_axis=0, concat_axis=0, tiled=True
        ).astype(p6.dtype),
        lax.all_to_all(
            p7.astype(jnp.bfloat16), "dp", split_axis=0, concat_axis=0, tiled=True
        ).astype(p7.dtype),
    )
    partial_value = tuple((jnp.sum(piece, axis=0) for piece in received))
    q0, q1, q2, q3, q4, q5, q6, q7 = partial_value
    gathered_parts = (
        lax.all_to_all(
            q0.astype(jnp.bfloat16), "fsdp", split_axis=0, concat_axis=0, tiled=True
        ).astype(q0.dtype),
        lax.all_to_all(
            q1.astype(jnp.bfloat16), "fsdp", split_axis=0, concat_axis=0, tiled=True
        ).astype(q1.dtype),
        lax.all_to_all(
            q2.astype(jnp.bfloat16), "fsdp", split_axis=0, concat_axis=0, tiled=True
        ).astype(q2.dtype),
        lax.all_to_all(
            q3.astype(jnp.bfloat16), "fsdp", split_axis=0, concat_axis=0, tiled=True
        ).astype(q3.dtype),
        lax.all_to_all(
            q4.astype(jnp.bfloat16), "fsdp", split_axis=0, concat_axis=0, tiled=True
        ).astype(q4.dtype),
        lax.all_to_all(
            q5.astype(jnp.bfloat16), "fsdp", split_axis=0, concat_axis=0, tiled=True
        ).astype(q5.dtype),
        lax.all_to_all(
            q6.astype(jnp.bfloat16), "fsdp", split_axis=0, concat_axis=0, tiled=True
        ).astype(q6.dtype),
        lax.all_to_all(
            q7.astype(jnp.bfloat16), "fsdp", split_axis=0, concat_axis=0, tiled=True
        ).astype(q7.dtype),
    )
    return tuple((jnp.sum(piece, axis=0) for piece in gathered_parts))


def on_device(
    tokens,
    image_tokens,
    caption_lengths,
    arrival_order,
    w_qkv,
    w_out,
    w_cross_q,
    w_cross_kv,
    w_cross_out,
    w_up,
    w_down,
    small_params,
    cotangent,
):
    lengths = caption_lengths[0]
    slot_rows = slot_index(lengths, arrival_order[0])
    captions = lengths.shape[0]
    slot_total = captions * CAP_LEN
    arrived, arrived_grad = (
        lax.all_to_all(tokens, "fsdp", split_axis=0, concat_axis=0, tiled=True),
        lax.all_to_all(cotangent, "fsdp", split_axis=0, concat_axis=0, tiled=True),
    )
    slotted = jnp.zeros((slot_total, D), jnp.float32).at[slot_rows].set(arrived.astype(jnp.float32))
    grad_slot = (
        jnp.zeros((slot_total, D), jnp.float32).at[slot_rows].set(arrived_grad.astype(jnp.float32))
    )
    positions = jnp.arange(CAP_LEN, dtype=jnp.int32)
    allowed = (positions[None, :] <= positions[:, None])[None, None] & (
        positions[None, None, None, :] < lengths[:, None, None, None]
    )
    open_mask = jnp.ones((1, 1, 1, 1), jnp.bool_)
    image_rows = image_tokens.reshape(-1, V)
    owned_shards = (w_qkv, w_out, w_cross_q, w_cross_kv, w_cross_out, w_up, w_down, small_params)
    params = unpack_params(
        (
            lax.all_gather(owned_shards[0], ("dp", "fsdp"), axis=0, tiled=True),
            lax.all_gather(owned_shards[1], ("dp", "fsdp"), axis=0, tiled=True),
            lax.all_gather(owned_shards[2], ("dp", "fsdp"), axis=0, tiled=True),
            lax.all_gather(owned_shards[3], ("dp", "fsdp"), axis=0, tiled=True),
            lax.all_gather(owned_shards[4], ("dp", "fsdp"), axis=0, tiled=True),
            lax.all_gather(owned_shards[5], ("dp", "fsdp"), axis=0, tiled=True),
            lax.all_gather(owned_shards[6], ("dp", "fsdp"), axis=0, tiled=True),
            lax.all_gather(owned_shards[7], ("dp", "fsdp"), axis=0, tiled=True),
        )
    )
    result, saved_state = forward(slotted, image_rows, params, allowed, open_mask)
    params_again = unpack_params(
        (
            lax.all_gather(owned_shards[0], ("dp", "fsdp"), axis=0, tiled=True),
            lax.all_gather(owned_shards[1], ("dp", "fsdp"), axis=0, tiled=True),
            lax.all_gather(owned_shards[2], ("dp", "fsdp"), axis=0, tiled=True),
            lax.all_gather(owned_shards[3], ("dp", "fsdp"), axis=0, tiled=True),
            lax.all_gather(owned_shards[4], ("dp", "fsdp"), axis=0, tiled=True),
            lax.all_gather(owned_shards[5], ("dp", "fsdp"), axis=0, tiled=True),
            lax.all_gather(owned_shards[6], ("dp", "fsdp"), axis=0, tiled=True),
            lax.all_gather(owned_shards[7], ("dp", "fsdp"), axis=0, tiled=True),
        )
    )
    _, state_again = forward(slotted, image_rows, params_again, allowed, open_mask)
    grad_input, grad_image, flat_grads = backward(
        state_again, grad_slot, image_rows, params_again, allowed, open_mask
    )
    summed = sum_to_owners(flat_grads)
    out_rows = result[slot_rows].astype(jnp.bfloat16)
    grad_rows = grad_input[slot_rows].astype(jnp.bfloat16)
    layer_out, grad_tokens = (
        lax.all_to_all(out_rows, "fsdp", split_axis=0, concat_axis=0, tiled=True),
        lax.all_to_all(grad_rows, "fsdp", split_axis=0, concat_axis=0, tiled=True),
    )
    return (layer_out, grad_tokens, grad_image.reshape(image_tokens.shape)) + tuple(summed)


def solution(mesh):
    return jax.shard_map(
        on_device,
        mesh=mesh,
        in_specs=(
            P(("dp", "fsdp"), None),
            P(("dp", "fsdp"), None, None),
            P(("dp", "fsdp"), None),
            P(("dp", "fsdp"), None),
            P(("dp", "fsdp")),
            P(("dp", "fsdp")),
            P(("dp", "fsdp")),
            P(("dp", "fsdp")),
            P(("dp", "fsdp")),
            P(("dp", "fsdp")),
            P(("dp", "fsdp")),
            P(("dp", "fsdp")),
            P(("dp", "fsdp"), None),
        ),
        out_specs=(
            P(("dp", "fsdp"), None),
            P(("dp", "fsdp"), None),
            P(("dp", "fsdp"), None, None),
            P(("dp", "fsdp")),
            P(("dp", "fsdp")),
            P(("dp", "fsdp")),
            P(("dp", "fsdp")),
            P(("dp", "fsdp")),
            P(("dp", "fsdp")),
            P(("dp", "fsdp")),
            P(("dp", "fsdp")),
        ),
        check_vma=False,
    )
```

profile of v0, /device:TPU:0, one launch (start us, length us, event | category | flops | bytes accessed | tf_op | source)
XLA Modules:
  0.0 1134.6 jit_solution(7460575959141492028)
XLA Ops:
  20.9 41.9 %all-reduce = bf16[8448]{0:T(1024)(128)(2,1)S(1)} all-reduce(bf16[8448]{0:T(1024)(128)(2,1)S(1)} %dynamic-update-slice), channel_id=1, replica_groups=mesh['dp'=8,'fsdp'=4] {'dp','fsdp'}, use_global_device_ids=true, to_apply=%add | all-reduce | flops 8448 | bytes 33792
  79.3 44.5 %all-gather.14.cloned.1.call-done = bf16[589824]{0:T(1024)(128)(2,1)} async-done(((bf16[18432]{0:T(1024)(128)(2,1)}), bf16[589824]{0:T(1024)(128)(2,1)}) %all-gather.14.cloned.1.call-update) | async-done | bytes 1179664 | tf_op jit(solution)/shard_map/all_gather | solution.py:402
  127.1 52.6 %all-gather.16.cloned.1.call-done = bf16[589824]{0:T(1024)(128)(2,1)} async-done(((bf16[18432]{0:T(1024)(128)(2,1)}), bf16[589824]{0:T(1024)(128)(2,1)}) %all-gather.16.cloned.1.call-update) | async-done | bytes 1179664 | tf_op jit(solution)/shard_map/all_gather | solution.py:404
  183.1 55.7 %all-gather.12.cloned.1.call-done = bf16[1179648]{0:T(1024)(128)(2,1)} async-done(((bf16[36864]{0:T(1024)(128)(2,1)}), bf16[1179648]{0:T(1024)(128)(2,1)}) %all-gather.12.cloned.1.call-update) | async-done | bytes 2359312 | tf_op jit(solution)/shard_map/all_gather | solution.py:403
  238.8 5.6 reshape.379
  244.4 5.6 convolution_convert_fusion.4
  250.0 4.7 copy.200
  254.7 6.2 reshape.380
  260.9 5.2 fusion.52
  266.1 34.6 %all-gather.8.cloned.1.call-done = bf16[1769472]{0:T(1024)(128)(2,1)} async-done(((bf16[55296]{0:T(1024)(128)(2,1)}), bf16[1769472]{0:T(1024)(128)(2,1)}) %all-gather.8.cloned.1.call-update) | async-done | bytes 3538960 | tf_op jit(solution)/shard_map/all_gather | solution.py:400
  300.6 7.6 reshape.374
  308.2 4.3 convolution_convert_fusion.3
  352.5 13.3 %all-gather.18.cloned.1.call-done = bf16[2359296]{0:T(1024)(128)(2,1)} async-done(((bf16[73728]{0:T(1024)(128)(2,1)}), bf16[2359296]{0:T(1024)(128)(2,1)}) %all-gather.18.cloned.1.call-update) | async-done | bytes 4718608 | tf_op jit(solution)/shard_map/all_gather | solution.py:405
  365.8 8.2 reshape.385
  374.0 11.9 %multiply_convert_fusion.2 = (bf16[256,3072]{1,0:T(8,128)(2,1)}, f32[256,3072]{1,0:T(8,128)}, f32[256,3072]{1,0:T(8,128)}) fusion(f32[3072]{0:T(1024)} %slice.103, bf16[768,3072]{1,0:T(8,128)(2,1)} %reshape.385, f32[256,768]{1,0:T(8,128)} %copy-done.8, f32[768]{0:T(1024)S(1)} %get-tuple-element.37, f32[768]{0:T(1024)S(1)} %get-tuple-element.36, ...), kind=kOutput, calls=%fused_computation.19 | convolution fusion | flops 1260847104 | bytes 13389824 | tf_op jit(solution)/shard_map/dot_general | solution.py:158
  385.9 45.3 %all-gather.20.cloned.1.call-done = bf16[2359296]{0:T(1024)(128)(2,1)} async-done(((bf16[73728]{0:T(1024)(128)(2,1)}), bf16[2359296]{0:T(1024)(128)(2,1)}) %all-gather.20.cloned.1.call-update) | async-done | bytes 4718608 | tf_op jit(solution)/shard_map/all_gather | solution.py:406
  431.2 9.5 reshape.386
  440.6 7.2 fusion.59
  447.8 5.1 multiply_reduce_fusion.3
  487.3 5.5 copy.222
  492.7 4.5 convert_element_type.283
  497.4 4.5 multiply_reduce_fusion.5
  505.0 4.3 all-to-all-start.18
  509.3 5.0 fusion.15
  548.6 6.4 all-to-all-start.12
  560.7 23.4 %all-to-all-done.12 = bf16[8,4,18432]{2,1,0:T(4,128)(2,1)} async-done(((bf16[8,4,18432]{2,1,0:T(4,128)(2,1)}), bf16[8,4,18432]{2,1,0:T(4,128)(2,1)}, u32[]{:S(2)}, u32[]{:S(2)}) %all-to-all-start.12) | async-done | bytes 1179680 | tf_op jit(solution)/shard_map/all_to_all | solution.py:320
  592.7 24.0 %all-to-all-done.8 = bf16[8,4,18432]{2,1,0:T(4,128)(2,1)} async-done(((bf16[8,4,18432]{2,1,0:T(4,128)(2,1)}), bf16[8,4,18432]{2,1,0:T(4,128)(2,1)}, u32[]{:S(2)}, u32[]{:S(2)}) %all-to-all-start.8) | async-done | bytes 1179680 | tf_op jit(solution)/shard_map/all_to_all | solution.py:314
  628.2 21.0 %all-to-all-done.6 = bf16[8,4,18432]{2,1,0:T(4,128)(2,1)} async-done(((bf16[8,4,18432]{2,1,0:T(4,128)(2,1)}), bf16[8,4,18432]{2,1,0:T(4,128)(2,1)}, u32[]{:S(2)}, u32[]{:S(2)}) %all-to-all-start.6) | async-done | bytes 1179680 | tf_op jit(solution)/shard_map/all_to_all | solution.py:311
  677.8 6.0 fusion.6
  683.8 4.3 copy.229
  688.0 4.7 convert_element_type.299
  692.7 4.5 all-to-all-start.10
  701.1 7.3 convert_element_type.289
  708.4 43.7 %all-to-all-done.10 = bf16[8,4,36864]{2,1,0:T(4,128)(2,1)} async-done(((bf16[8,4,36864]{2,1,0:T(4,128)(2,1)}), bf16[8,4,36864]{2,1,0:T(4,128)(2,1)}, u32[]{:S(2)}, u32[]{:S(2)}) %all-to-all-start.10) | async-done | bytes 2359328 | tf_op jit(solution)/shard_map/all_to_all | solution.py:317
  752.0 4.5 all-to-all-start.4
  761.4 74.4 %all-to-all-done.4 = bf16[8,4,55296]{2,1,0:T(4,128)(2,1)} async-done(((bf16[8,4,55296]{2,1,0:T(4,128)(2,1)}), bf16[8,4,55296]{2,1,0:T(4,128)(2,1)}, u32[]{:S(2)}, u32[]{:S(2)}) %all-to-all-start.4) | async-done | bytes 3538976 | tf_op jit(solution)/shard_map/all_to_all | solution.py:308
  849.1 5.1 convolution_convert_fusion.1
  854.2 8.3 convert_element_type.305
  863.3 4.8 all-to-all-start.14
  868.2 5.0 convolution_convert_fusion
  873.1 8.2 convert_element_type.308
  881.4 92.1 %all-to-all-done.14 = bf16[8,4,73728]{2,1,0:T(4,128)(2,1)} async-done(((bf16[8,4,73728]{2,1,0:T(4,128)(2,1)}), bf16[8,4,73728]{2,1,0:T(4,128)(2,1)}, u32[]{:S(2)}, u32[]{:S(2)}) %all-to-all-start.14) | async-done | bytes 4718624 | tf_op jit(solution)/shard_map/all_to_all | solution.py:323
  973.4 4.6 all-to-all-start.16
  978.1 6.5 convolution_convert_fusion.7
  989.6 4.7 reduce_sum.463
  997.1 85.5 %all-to-all-done.16 = bf16[8,4,73728]{2,1,0:T(4,128)(2,1)} async-done(((bf16[8,4,73728]{2,1,0:T(4,128)(2,1)}), bf16[8,4,73728]{2,1,0:T(4,128)(2,1)}, u32[]{:S(2)}, u32[]{:S(2)}) %all-to-all-start.16) | async-done | bytes 4718624 | tf_op jit(solution)/shard_map/all_to_all | solution.py:326
  1095.2 5.5 reduce_sum.468
  1115.7 4.5 all-to-all-done.17
  (357 shorter events, 267.2 us)
Async XLA Ops:
  7.2 237.2 %copy-start = (bf16[4,256,768]{2,1,0:T(8,128)(2,1)S(1)}, bf16[4,256,768]{2,1,0:T(8,128)(2,1)}, u32[]{:S(2)}) copy-start(bf16[4,256,768]{2,1,0:T(8,128)(2,1)} %param.14) | copy-start | bytes 4718596
  7.2 68.8 %all-gather.10.cloned.1.call-start = ((), (), s32[]{:S(2)}) async-start(), calls=%async_computation.21 | async-start | bytes 1216512 | tf_op jit(solution)/shard_map/all_gather | solution.py:401
  7.9 115.9 %all-gather.14.cloned.1.call-start = ((), (), s32[]{:S(2)}) async-start(), calls=%async_computation.23 | async-start | bytes 1216512 | tf_op jit(solution)/shard_map/all_gather | solution.py:402
  8.7 171.1 %all-gather.16.cloned.1.call-start = ((), (), s32[]{:S(2)}) async-start(), calls=%async_computation.24 | async-start | bytes 1216512 | tf_op jit(solution)/shard_map/all_gather | solution.py:404
  9.4 229.4 %all-gather.12.cloned.1.call-start = ((), (), s32[]{:S(2)}) async-start(), calls=%async_computation.22 | async-start | bytes 2433024 | tf_op jit(solution)/shard_map/all_gather | solution.py:403
  10.0 290.6 %all-gather.8.cloned.1.call-start = ((), (), s32[]{:S(2)}) async-start(), calls=%async_computation.20 | async-start | bytes 3649536 | tf_op jit(solution)/shard_map/all_gather | solution.py:400
  10.6 355.2 %all-gather.18.cloned.1.call-start = ((), (), s32[]{:S(2)}) async-start(), calls=%async_computation.25 | async-start | bytes 4866048 | tf_op jit(solution)/shard_map/all_gather | solution.py:405
  11.2 52.8 %all-to-all-start = ((bf16[4,40,768]{2,1,0:T(8,128)(2,1)}), bf16[4,40,768]{2,1,0:T(8,128)(2,1)S(1)}, u32[]{:S(2)}, u32[]{:S(2)}) async-start(bf16[4,40,768]{2,1,0:T(8,128)(2,1)} %bitcast.178), calls=%async_computation | async-start | bytes 491520 | tf_op jit(solution)/shard_map/all_to_all | solution.py:384
  15.4 415.8 %all-gather.20.cloned.1.call-start = ((), (), s32[]{:S(2)}) async-start(), calls=%async_computation.26 | async-start | bytes 4866048 | tf_op jit(solution)/shard_map/all_gather | solution.py:406
  64.0 9.4 all-to-all-start.2
  69.5 238.7 %copy-start.3 = (f32[256,768]{1,0:T(8,128)}, f32[256,768]{1,0:T(8,128)S(1)}, u32[]{:S(2)}) copy-start(f32[256,768]{1,0:T(8,128)S(1)} %scatter_custom_fusion) | copy-start | bytes 2359300
  75.7 232.6 %copy-start.54 = (f32[256]{0:T(256)}, f32[256]{0:T(256)S(1)}, u32[]{:S(2)}) copy-start(f32[256]{0:T(256)S(1)} %broadcast_multiply_fusion.2) | copy-start | bytes 3076
  75.9 107.2 %copy-start.71 = (f32[256]{0:T(256)}, f32[256]{0:T(256)S(1)}, u32[]{:S(2)}) copy-start(f32[256]{0:T(256)S(1)} %multiply_reduce_fusion.11) | copy-start | bytes 3076
  75.9 232.3 %copy-start.64 = (f32[256]{0:T(256)}, f32[256]{0:T(256)S(1)}, u32[]{:S(2)}) copy-start(f32[256]{0:T(256)S(1)} %fusion.42) | copy-start | bytes 3076
  347.9 26.0 %copy-start.34 = (bf16[256,768]{0,1:T(8,128)(2,1)}, bf16[256,768]{0,1:T(8,128)(2,1)S(1)}, u32[]{:S(2)}) copy-start(bf16[256,768]{0,1:T(8,128)(2,1)S(1)} %reshape.383) | copy-start | bytes 1179652
  487.3 10.0 copy-start.4
  487.3 10.0 copy-start.55
  487.3 10.0 copy-start.65
  497.4 11.9 %copy-start.10 = (f32[256,768]{1,0:T(8,128)S(1)}, f32[256,768]{1,0:T(8,128)}, u32[]{:S(2)}) copy-start(f32[256,768]{1,0:T(8,128)} %copy-done.8) | copy-start | bytes 2359300
  497.4 11.9 %copy-start.80 = (f32[768]{0:T(1024)S(1)}, f32[768]{0:T(1024)}, u32[]{:S(2)}) copy-start(f32[768]{0:T(1024)} %get-tuple-element.35) | copy-start | bytes 9220
  505.0 11.1 all-to-all-start.18
  514.3 11.9 %copy-start.20 = (bf16[256,768]{1,0:T(8,128)(2,1)S(1)}, bf16[256,768]{1,0:T(8,128)(2,1)}, u32[]{:S(2)}) copy-start(bf16[256,768]{1,0:T(8,128)(2,1)} %fusion.15) | copy-start | bytes 1179652
  514.3 18.4 %copy-start.16 = (f32[256,768]{1,0:T(8,128)S(1)}, f32[256,768]{1,0:T(8,128)}, u32[]{:S(2)}) copy-start(f32[256,768]{1,0:T(8,128)} %copy-done.15) | copy-start | bytes 2359300
  521.2 7.5 all-to-all-start.19
  528.7 10.0 all-to-all-start.1
  538.7 9.2 all-to-all-start.3
  542.1 13.0 %copy-start.7 = (f32[256,768]{1,0:T(8,128)S(1)}, f32[256,768]{1,0:T(8,128)}, u32[]{:S(2)}) copy-start(f32[256,768]{1,0:T(8,128)} %copy-done.5) | copy-start | bytes 2359300
  548.6 35.5 %all-to-all-start.12 = ((bf16[8,4,18432]{2,1,0:T(4,128)(2,1)}), bf16[8,4,18432]{2,1,0:T(4,128)(2,1)}, u32[]{:S(2)}, u32[]{:S(2)}) async-start(bf16[8,4,18432]{2,1,0:T(4,128)(2,1)} %convert_element_type.302), calls=%async_computation.12 | async-start | bytes 2359296 | tf_op jit(solution)/shard_map/all_to_all | solution.py:320
  555.1 33.3 %copy-start.33 = (bf16[256,768]{0,1:T(8,128)(2,1)S(1)}, bf16[256,768]{0,1:T(8,128)(2,1)}, u32[]{:S(2)}) copy-start(bf16[256,768]{0,1:T(8,128)(2,1)} %copy-done.32) | copy-start | bytes 1179652
  557.8 30.5 %copy-start.17 = (f32[256,768]{1,0:T(8,128)S(1)}, f32[256,768]{1,0:T(8,128)}, u32[]{:S(2)}) copy-start(f32[256,768]{1,0:T(8,128)} %copy-done.15) | copy-start | bytes 2359300
  584.1 32.6 %all-to-all-start.8 = ((bf16[8,4,18432]{2,1,0:T(4,128)(2,1)}), bf16[8,4,18432]{2,1,0:T(4,128)(2,1)}, u32[]{:S(2)}, u32[]{:S(2)}) async-start(bf16[8,4,18432]{2,1,0:T(4,128)(2,1)} %convert_element_type.295), calls=%async_computation.8 | async-start | bytes 2359296 | tf_op jit(solution)/shard_map/all_to_all | solution.py:314
  589.8 31.1 %copy-start.26 = (bf16[4,64,12,64]{1,3,2,0:T(8,128)(2,1)S(1)}, bf16[4,64,12,64]{1,3,2,0:T(8,128)(2,1)}, u32[]{:S(2)}) copy-start(bf16[4,64,12,64]{1,3,2,0:T(8,128)(2,1)} %copy.224) | copy-start | bytes 1179652
  589.8 31.1 %copy-start.44 = (f32[4,12,64]{2,1,0:T(8,128)S(1)}, f32[4,12,64]{2,1,0:T(8,128)}, u32[]{:S(2)}) copy-start(f32[4,12,64]{2,1,0:T(8,128)} %copy-done.42) | copy-start | bytes 36868
  616.7 32.5 %all-to-all-start.6 = ((bf16[8,4,18432]{2,1,0:T(4,128)(2,1)}), bf16[8,4,18432]{2,1,0:T(4,128)(2,1)}, u32[]{:S(2)}, u32[]{:S(2)}) async-start(bf16[8,4,18432]{2,1,0:T(4,128)(2,1)} %convert_element_type.292), calls=%async_computation.6 | async-start | bytes 2359296 | tf_op jit(solution)/shard_map/all_to_all | solution.py:311
  649.2 10.1 all-to-all-start.13
  659.4 14.3 %all-to-all-start.9 = ((bf16[4,2,9216]{2,1,0:T(2,128)(2,1)}), bf16[4,2,9216]{2,1,0:T(2,128)(2,1)S(1)}, u32[]{:S(2)}, u32[]{:S(2)}) async-start(bf16[4,2,9216]{2,1,0:T(2,128)(2,1)} %reshape.437), calls=%async_computation.9 | async-start | bytes 294912 | tf_op jit(solution)/shard_map/all_to_all | solution.py:342
  673.6 10.1 copy-start.50
  673.6 19.1 %all-to-all-start.7 = ((bf16[4,2,9216]{2,1,0:T(2,128)(2,1)}), bf16[4,2,9216]{2,1,0:T(2,128)(2,1)}, u32[]{:S(2)}, u32[]{:S(2)}) async-start(bf16[4,2,9216]{2,1,0:T(2,128)(2,1)} %reshape.435), calls=%async_computation.7 | async-start | bytes 294912 | tf_op jit(solution)/shard_map/all_to_all | solution.py:339
  692.7 59.3 %all-to-all-start.10 = ((bf16[8,4,36864]{2,1,0:T(4,128)(2,1)}), bf16[8,4,36864]{2,1,0:T(4,128)(2,1)}, u32[]{:S(2)}, u32[]{:S(2)}) async-start(bf16[8,4,36864]{2,1,0:T(4,128)(2,1)} %convert_element_type.299), calls=%async_computation.10 | async-start | bytes 4718592 | tf_op jit(solution)/shard_map/all_to_all | solution.py:317
  752.0 83.8 %all-to-all-start.4 = ((bf16[8,4,55296]{2,1,0:T(4,128)(2,1)}), bf16[8,4,55296]{2,1,0:T(4,128)(2,1)}, u32[]{:S(2)}, u32[]{:S(2)}) async-start(bf16[8,4,55296]{2,1,0:T(4,128)(2,1)} %convert_element_type.289), calls=%async_computation.4 | async-start | bytes 7077888 | tf_op jit(solution)/shard_map/all_to_all | solution.py:308
  835.8 9.8 all-to-all-start.11
  839.2 9.8 copy-start.11
  845.6 17.0 %all-to-all-start.5 = ((bf16[4,2,27648]{2,1,0:T(2,128)(2,1)}), bf16[4,2,27648]{2,1,0:T(2,128)(2,1)S(1)}, u32[]{:S(2)}, u32[]{:S(2)}) async-start(bf16[4,2,27648]{2,1,0:T(2,128)(2,1)} %reshape.433), calls=%async_computation.5 | async-start | bytes 884736 | tf_op jit(solution)/shard_map/all_to_all | solution.py:336
  863.3 110.1 %all-to-all-start.14 = ((bf16[8,4,73728]{2,1,0:T(4,128)(2,1)}), bf16[8,4,73728]{2,1,0:T(4,128)(2,1)}, u32[]{:S(2)}, u32[]{:S(2)}) async-start(bf16[8,4,73728]{2,1,0:T(4,128)(2,1)} %convert_element_type.305), calls=%async_computation.14 | async-start | bytes 9437184 | tf_op jit(solution)/shard_map/all_to_all | solution.py:323
  973.4 109.1 %all-to-all-start.16 = ((bf16[8,4,73728]{2,1,0:T(4,128)(2,1)}), bf16[8,4,73728]{2,1,0:T(4,128)(2,1)}, u32[]{:S(2)}, u32[]{:S(2)}) async-start(bf16[8,4,73728]{2,1,0:T(4,128)(2,1)} %convert_element_type.308), calls=%async_computation.16 | async-start | bytes 9437184 | tf_op jit(solution)/shard_map/all_to_all | solution.py:326
  1082.6 23.8 %all-to-all-start.15 = ((bf16[4,2,36864]{2,1,0:T(2,128)(2,1)}), bf16[4,2,36864]{2,1,0:T(2,128)(2,1)S(1)}, u32[]{:S(2)}, u32[]{:S(2)}) async-start(bf16[4,2,36864]{2,1,0:T(2,128)(2,1)} %reshape.443), calls=%async_computation.15 | async-start | bytes 1179648 | tf_op jit(solution)/shard_map/all_to_all | solution.py:351
  1106.4 13.8 %all-to-all-start.17 = ((bf16[4,2,36864]{2,1,0:T(2,128)(2,1)}), bf16[4,2,36864]{2,1,0:T(2,128)(2,1)}, u32[]{:S(2)}, u32[]{:S(2)}) async-start(bf16[4,2,36864]{2,1,0:T(2,128)(2,1)} %reshape.445), calls=%async_computation.17 | async-start | bytes 1179648 | tf_op jit(solution)/shard_map/all_to_all | solution.py:354
  1113.1 13.5 %copy-start.41 = (bf16[4,40,768]{2,1,0:T(8,128)(2,1)S(1)}, bf16[4,40,768]{2,1,0:T(8,128)(2,1)}, u32[]{:S(2)}) copy-start(bf16[4,40,768]{2,1,0:T(8,128)(2,1)} %copy-done.40) | copy-start | bytes 737284
  (64 other events, 246.5 us)
Sparse Core Ops, SparseCore 0:
  10.9 56.8 all-gather.9
  70.8 52.9 all-gather.13
  126.7 53.0 all-gather.15
  182.5 56.2 all-gather.11
  241.6 59.0 all-gather.7
  303.4 62.3 all-gather.17
  368.7 62.3 all-gather.19
where the time goes:
time: 1140 us; the launch traced here: 1130 us
  waiting for transfers between devices  627 us (55%)
  local copies, waits for them, and re-layouts  187 us (16%)
  matrix products  109 us (10%)
  starting transfers between devices  82.5 us (7%)
  other arithmetic  71.9 us (6%)
  blocking collectives  41.9 us (4%)
  between operations  15.9 us (1%)
    all_to_all x1, waiting for transfers between devices, sum_to_owners(): lax.all_to_all(p5.astype(jnp.bfloat16), 'dp', split_axis=0, concat_axis=0...  92.1 us
    all_to_all x1, waiting for transfers between devices, sum_to_owners(): lax.all_to_all(p6.astype(jnp.bfloat16), 'dp', split_axis=0, concat_axis=0...  85.5 us
    all_to_all x1, waiting for transfers between devices, sum_to_owners(): lax.all_to_all(p0.astype(jnp.bfloat16), 'dp', split_axis=0, concat_axis=0...  74.4 us
    all_gather x1, waiting for transfers between devices, on_device(): lax.all_gather(owned_shards[3], ('dp', 'fsdp'), axis=0, tiled=True)  55.7 us
    all_gather x1, waiting for transfers between devices, on_device(): lax.all_gather(owned_shards[4], ('dp', 'fsdp'), axis=0, tiled=True)  52.6 us
    all_gather x1, waiting for transfers between devices, on_device(): lax.all_gather(owned_shards[6], ('dp', 'fsdp'), axis=0, tiled=True)  45.3 us
    all_gather x1, waiting for transfers between devices, on_device(): lax.all_gather(owned_shards[2], ('dp', 'fsdp'), axis=0, tiled=True)  44.5 us
    all_to_all x1, waiting for transfers between devices, sum_to_owners(): lax.all_to_all(p3.astype(jnp.bfloat16), 'dp', split_axis=0, concat_axis=0...  43.7 us
  transfers between devices with their start and end apart: 27, of which 19 were waited for; matrix products, arithmetic and copies ran while one was open for 24% of the time, Pallas kernels for 0%

commit v1 on v0

v1 whole, which is shorter than its diff:
```python
import functools

import jax
import jax.numpy as jnp
from jax import lax
from jax.experimental import pallas as pl
from jax.experimental.pallas import tpu as pltpu
from jax.sharding import Mesh
from jax.sharding import PartitionSpec as P

D = 768
HEAD_DIM = 64
FF = 3072
IMG = 256
CAP_LEN = 64
LANES = 128
PAIRS = D // LANES
FOLD = FF // D
SCALE = HEAD_DIM ** (-0.5)
epsilon = 1e-05
masked_fill = 1e30

BF = jnp.bfloat16
F32 = jnp.float32
AXES = ("z", "x", "y", "c")
COLS = {}
_at = 0
for _name, _width in (
    ("qkv", 3 * D),
    ("out", D),
    ("cross_q", D),
    ("cross_kv", 2 * D),
    ("cross_out", D),
    ("up", FF),
    ("down", FF),
):
    COLS[_name] = (_at, _width)
    _at += _width
TOTAL_COLS = _at


def mm(a, b):
    return lax.dot_general(a, b, (((1,), (0,)), ((), ())), preferred_element_type=F32)


def mm_t(a, b):
    return lax.dot_general(a, b, (((1,), (1,)), ((), ())), preferred_element_type=F32)


def t_mm(a, b):
    return lax.dot_general(a, b, (((0,), (0,)), ((), ())), preferred_element_type=F32)


def norm_rows(inputs, gain_vec, shift_vec):
    centred = inputs - jnp.mean(inputs, axis=-1, keepdims=True)
    variance = jnp.mean(centred * centred, axis=-1, keepdims=True)
    return centred * lax.rsqrt(variance + epsilon) * gain_vec + shift_vec


def norm_back(inputs, gain_vec, grad_normed):
    centred = inputs - jnp.mean(inputs, axis=-1, keepdims=True)
    variance = jnp.mean(centred * centred, axis=-1, keepdims=True)
    scale = lax.rsqrt(variance + epsilon)
    unit = centred * scale
    weighted = grad_normed * gain_vec
    grad_in = scale * (
        weighted
        - jnp.mean(weighted, axis=-1, keepdims=True)
        - unit * jnp.mean(weighted * unit, axis=-1, keepdims=True)
    )
    grad_gain = jnp.sum(grad_normed * unit, axis=0, keepdims=True)
    grad_shift = jnp.sum(grad_normed, axis=0, keepdims=True)
    return grad_in, grad_gain, grad_shift


def arrival_pick(arr_ref):
    rows = arr_ref.shape[1]
    place = lax.broadcasted_iota(jnp.int32, (rows, rows), 0)
    return jnp.where(place == arr_ref[...], 1.0, 0.0).astype(BF)


def caption_of(index, lens_ref):
    end = jnp.int32(0)
    found = jnp.zeros_like(index)
    for c in range(lens_ref.shape[1] - 1):
        end = end + lens_ref[0, c]
        found = found + jnp.where(index >= end, 1, 0)
    return found


def slot_pick(lens_ref, rows):
    captions = lens_ref.shape[1]
    shape = (captions * CAP_LEN, rows)
    slot = lax.broadcasted_iota(jnp.int32, shape, 0)
    row = lax.broadcasted_iota(jnp.int32, shape, 1)
    start = jnp.int32(0)
    hit = jnp.zeros(shape, F32)
    for c in range(captions):
        length = lens_ref[0, c]
        inside = slot - c * CAP_LEN
        ok = (inside >= 0) & (inside < length) & (row - start == inside)
        hit = hit + jnp.where(ok, 1.0, 0.0)
        start = start + length
    return hit.astype(BF)


def pair_mask(rows):
    shape = (2 * rows, LANES)
    top = lax.broadcasted_iota(jnp.int32, shape, 0) < rows
    left = lax.broadcasted_iota(jnp.int32, shape, 1) < HEAD_DIM
    return jnp.where(top == left, 1.0, 0.0).astype(BF)


def stack_pair(block, mask):
    return jnp.concatenate([block, block], axis=0) * mask


def merge_pair(stacked):
    rows = stacked.shape[0] // 2
    left = lax.broadcasted_iota(jnp.int32, (rows, LANES), 1) < HEAD_DIM
    return jnp.where(left, stacked[:rows], stacked[rows:])


def softmax_rows(scores):
    shifted = jnp.exp(scores - jnp.max(scores, axis=-1, keepdims=True))
    return shifted / jnp.sum(shifted, axis=-1, keepdims=True)


def load_cols(weights_ref, name, target, sem):
    at, width = COLS[name]
    copy = pltpu.make_async_copy(weights_ref.at[:, pl.ds(at, width)], target, sem)
    copy.start()
    return copy


def place_kernel(arr, tok, cot, table, slotted, normed, grad_slot):
    pick = arrival_pick(arr)
    rows = mm(pick, tok[...])
    slotted[...] = rows.astype(BF)
    normed[...] = norm_rows(rows, table[0:1, :], table[3:4, :]).astype(BF)
    grad_slot[...] = mm(pick, cot[...]).astype(BF)


def kv_kernel(img, weights, kv, w_kv, sem):
    copy = load_cols(weights, "cross_kv", w_kv, sem.at[0])
    copy.wait()
    for c in range(img.shape[0] // IMG):
        rows = pl.ds(c * IMG, IMG)
        kv[rows, :] = mm(img[rows, :], w_kv[...]).astype(BF)


def self_kernel(
    lens, slotted, normed, table, weights,
    projected, probs, mixed, after_self, normed_cross, query_slots,
    w_qkv, w_out, w_cq, sem,
):
    copies = [
        load_cols(weights, "qkv", w_qkv, sem.at[0]),
        load_cols(weights, "out", w_out, sem.at[1]),
        load_cols(weights, "cross_q", w_cq, sem.at[2]),
    ]
    rows = slotted.shape[0]
    copies[0].wait()
    projected[...] = mm(normed[...], w_qkv[...]).astype(BF)
    place = lax.broadcasted_iota(jnp.int32, (2 * rows, rows), 0)
    query_at = jnp.where(place >= rows, place - rows, place)
    key_at = lax.broadcasted_iota(jnp.int32, (2 * rows, rows), 1)
    allowed = (caption_of(query_at, lens) == caption_of(key_at, lens)) & (key_at <= query_at)
    mask = pair_mask(rows)
    for p in range(PAIRS):
        cols = slice(p * LANES, (p + 1) * LANES)
        query = stack_pair(projected[:, cols], mask)
        key = projected[:, D + p * LANES : D + (p + 1) * LANES]
        value = projected[:, 2 * D + p * LANES : 2 * D + (p + 1) * LANES]
        scores = jnp.where(allowed, mm_t(query, key) * SCALE, -masked_fill)
        weights_low = softmax_rows(scores).astype(BF)
        probs[p] = weights_low
        mixed[:, cols] = merge_pair(mm(weights_low, value)).astype(BF)
    copies[1].wait()
    state = slotted[...].astype(F32) + mm(mixed[...], w_out[...])
    after_self[...] = state
    low = norm_rows(state, table[1:2, :], table[4:5, :]).astype(BF)
    normed_cross[...] = low
    copies[2].wait()
    query = mm(low, w_cq[...]).astype(BF)
    query_slots[...] = mm(slot_pick(lens, rows), query).astype(BF)


def cross_kernel(
    lens, query_slots, kv, after_self, table, weights,
    probs, mixed, after_cross, normed_mlp,
    w_co, mixed_slots, sem,
):
    copy = load_cols(weights, "cross_out", w_co, sem.at[0])
    rows = after_self.shape[0]
    mask = pair_mask(CAP_LEN)
    for c in range(lens.shape[1]):
        slots = slice(c * CAP_LEN, (c + 1) * CAP_LEN)
        images = slice(c * IMG, (c + 1) * IMG)
        for p in range(PAIRS):
            cols = slice(p * LANES, (p + 1) * LANES)
            query = stack_pair(query_slots[slots, cols], mask)
            scores = mm_t(query, kv[images, cols]) * SCALE
            weights_low = softmax_rows(scores).astype(BF)
            probs[c * PAIRS + p] = weights_low
            value = kv[images, D + p * LANES : D + (p + 1) * LANES]
            mixed_slots[slots, cols] = merge_pair(mm(weights_low, value)).astype(BF)
    low = t_mm(slot_pick(lens, rows), mixed_slots[...]).astype(BF)
    mixed[...] = low
    copy.wait()
    state = after_self[...] + mm(low, w_co[...])
    after_cross[...] = state
    normed_mlp[...] = norm_rows(state, table[2:3, :], table[5:6, :]).astype(BF)


def mlp_kernel(
    arr, after_cross, normed_mlp, grad_slot, table, weights,
    active, grad_hidden, layer_rows, grad_after, small,
    w_up, w_down, sem,
):
    copies = []
    for j in range(FOLD):
        for k, (name, target) in enumerate((("up", w_up), ("down", w_down))):
            at = COLS[name][0] + j * D
            copy = pltpu.make_async_copy(
                weights.at[:, pl.ds(at, D)], target.at[j], sem.at[2 * j + k]
            )
            copy.start()
            copies.append(copy)
    low = normed_mlp[...]
    grad_low = grad_slot[...]
    result = after_cross[...] + table[10:11, :]
    grad_normed = jnp.zeros(result.shape, F32)
    for j in range(FOLD):
        cols = slice(j * D, (j + 1) * D)
        copies[2 * j].wait()
        hidden = mm(low, w_up[j]) + table[6 + j : 7 + j, :]
        half = 0.5 + 0.5 * lax.erf(hidden * (0.5**0.5))
        act = (hidden * half).astype(BF)
        active[:, cols] = act
        slope = half + hidden * (jnp.exp(hidden * hidden * -0.5) * 0.3989422804014327)
        copies[2 * j + 1].wait()
        result = result + mm(act, w_down[j])
        grad_hid = (mm_t(grad_low, w_down[j]) * slope).astype(BF)
        grad_hidden[:, cols] = grad_hid
        small[2 + j : 3 + j, :] = jnp.sum(grad_hid.astype(F32), axis=0, keepdims=True)
        grad_normed = grad_normed + mm_t(grad_hid, w_up[j])
    layer_rows[...] = t_mm(arrival_pick(arr), result.astype(BF)).astype(BF)
    grad_full = grad_low.astype(F32)
    grad_in, grad_gain, grad_shift = norm_back(after_cross[...], table[2:3, :], grad_normed)
    grad_after[...] = grad_full + grad_in
    small[0:1, :] = grad_gain
    small[1:2, :] = grad_shift
    small[6:7, :] = jnp.sum(grad_full, axis=0, keepdims=True)
    small[7:8, :] = jnp.zeros_like(grad_gain)


def cross_back_kernel(
    lens, grad_after, probs, query_slots, kv, after_self, table, weights,
    grad_branch, grad_query, grad_kv, grad_state, small,
    w_co, w_cq, mixed_slots, query_grad_slots, sem,
):
    copies = [
        load_cols(weights, "cross_out", w_co, sem.at[0]),
        load_cols(weights, "cross_q", w_cq, sem.at[1]),
    ]
    rows = after_self.shape[0]
    branch = grad_after[...].astype(BF)
    grad_branch[...] = branch
    pick = slot_pick(lens, rows)
    copies[0].wait()
    mixed_slots[...] = mm(pick, mm_t(branch, w_co[...]).astype(BF)).astype(BF)
    mask = pair_mask(CAP_LEN)
    for c in range(lens.shape[1]):
        slots = slice(c * CAP_LEN, (c + 1) * CAP_LEN)
        images = slice(c * IMG, (c + 1) * IMG)
        for p in range(PAIRS):
            cols = slice(p * LANES, (p + 1) * LANES)
            value_cols = slice(D + p * LANES, D + (p + 1) * LANES)
            grad_mixed = stack_pair(mixed_slots[slots, cols], mask)
            query = stack_pair(query_slots[slots, cols], mask)
            weights_low = probs[c * PAIRS + p]
            attn = weights_low.astype(F32)
            grad_weights = mm_t(grad_mixed, kv[images, value_cols])
            centre = jnp.sum(attn * grad_weights, axis=-1, keepdims=True)
            grad_scores = (attn * (grad_weights - centre)).astype(BF)
            query_grad_slots[slots, cols] = (
                merge_pair(mm(grad_scores, kv[images, cols])) * SCALE
            ).astype(BF)
            grad_kv[images, cols] = (t_mm(grad_scores, query) * SCALE).astype(BF)
            grad_kv[images, value_cols] = t_mm(weights_low, grad_mixed).astype(BF)
    query_low = t_mm(pick, query_grad_slots[...]).astype(BF)
    grad_query[...] = query_low
    copies[1].wait()
    grad_in, grad_gain, grad_shift = norm_back(
        after_self[...], table[1:2, :], mm_t(query_low, w_cq[...])
    )
    grad_state[...] = grad_after[...] + grad_in
    small[0:1, :] = grad_gain
    small[1:2, :] = grad_shift
    small[2:8, :] = jnp.zeros((6, D), F32)


def self_back_kernel(
    arr, grad_state, probs, projected, slotted, table, weights,
    grad_branch, grad_projected, token_rows, small,
    w_out, w_qkv, mixed, sem,
):
    copies = [
        load_cols(weights, "out", w_out, sem.at[0]),
        load_cols(weights, "qkv", w_qkv, sem.at[1]),
    ]
    rows = slotted.shape[0]
    branch = grad_state[...].astype(BF)
    grad_branch[...] = branch
    copies[0].wait()
    mixed[...] = mm_t(branch, w_out[...]).astype(BF)
    mask = pair_mask(rows)
    for p in range(PAIRS):
        cols = slice(p * LANES, (p + 1) * LANES)
        key_cols = slice(D + p * LANES, D + (p + 1) * LANES)
        value_cols = slice(2 * D + p * LANES, 2 * D + (p + 1) * LANES)
        grad_mixed = stack_pair(mixed[:, cols], mask)
        query = stack_pair(projected[:, cols], mask)
        weights_low = probs[p]
        attn = weights_low.astype(F32)
        grad_weights = mm_t(grad_mixed, projected[:, value_cols])
        centre = jnp.sum(attn * grad_weights, axis=-1, keepdims=True)
        grad_scores = (attn * (grad_weights - centre)).astype(BF)
        grad_projected[:, cols] = (
            merge_pair(mm(grad_scores, projected[:, key_cols])) * SCALE
        ).astype(BF)
        grad_projected[:, key_cols] = (t_mm(grad_scores, query) * SCALE).astype(BF)
        grad_projected[:, value_cols] = t_mm(weights_low, grad_mixed).astype(BF)
    copies[1].wait()
    grad_in, grad_gain, grad_shift = norm_back(
        slotted[...].astype(F32), table[0:1, :], mm_t(grad_projected[...], w_qkv[...])
    )
    grad_slotted = (grad_state[...] + grad_in).astype(BF)
    token_rows[...] = t_mm(arrival_pick(arr), grad_slotted).astype(BF)
    small[0:1, :] = grad_gain
    small[1:2, :] = grad_shift
    small[2:8, :] = jnp.zeros((6, D), F32)


def put_blocks(grads, me, keep, send, at, first):
    _, _, nz, height, _ = keep.shape
    width = grads.shape[1]
    own_x, own_y, own_c = me[0, 1], me[0, 2], me[0, 3]
    for z in range(nz):
        for x in range(2):
            for y in range(2):
                low = (((z * 2 + x) * 2 + y) * 2) * height
                even = grads[low : low + height, :]
                odd = grads[low + height : low + 2 * height, :]
                far_x, far_y = lax.bitwise_xor(own_x, x), lax.bitwise_xor(own_y, y)
                i, j = (far_x, far_y) if first == "x" else (far_y, far_x)
                keep[i, j, z, :, at : at + width] = jnp.where(own_c == 0, even, odd).astype(BF)
                send[i, j, z, :, at : at + width] = jnp.where(own_c == 0, odd, even).astype(BF)


def weight_grad_kernel(first, pieces, me, *refs):
    keep, send = refs[-2:]
    for left, left_at, right, right_at, width, at in pieces:
        for lo in range(0, width, D):
            grads = t_mm(
                refs[left][:, left_at : left_at + D],
                refs[right][:, right_at + lo : right_at + lo + D],
            )
            put_blocks(grads, me, keep, send, at + lo, first)


def image_grad_kernel(grad_kv, weights, grad_image, w_kv, sem):
    copy = load_cols(weights, "cross_kv", w_kv, sem.at[0])
    copy.wait()
    for c in range(grad_kv.shape[0] // IMG):
        rows = pl.ds(c * IMG, IMG)
        grad_image[rows, :] = mm_t(grad_kv[rows, :], w_kv[...]).astype(BF)


VM = pl.BlockSpec(memory_space=pltpu.VMEM)
SM = pl.BlockSpec(memory_space=pltpu.SMEM)
HB = pl.BlockSpec(memory_space=pl.ANY)


def run(kernel, outs, specs, scratch, flops, *args, mib=44):
    shapes = [jax.ShapeDtypeStruct(s, t) for s, t in outs]
    moved = sum(a.size * a.dtype.itemsize for a in args) + sum(
        s.size * s.dtype.itemsize for s in shapes
    )
    return pl.pallas_call(
        kernel,
        out_shape=shapes,
        in_specs=specs,
        out_specs=[VM] * len(shapes),
        scratch_shapes=scratch,
        compiler_params=pltpu.CompilerParams(vmem_limit_bytes=mib * 2**20),
        cost_estimate=pl.CostEstimate(flops=flops, bytes_accessed=moved, transcendentals=0),
    )(*args)


def flip(value, axis):
    return lax.ppermute(value, axis, [(0, 1), (1, 0)])


def swap_all(value, axes):
    return lax.all_to_all(value, axes, split_axis=0, concat_axis=0, tiled=True)


def reduce_unit(keep, send, first, second):
    far = flip(send, "c").astype(F32)
    near = keep.astype(F32)
    one = flip((near[1] + far[1]).astype(BF), first).astype(F32)
    two = flip((near[0, 1] + far[0, 1] + one[1]).astype(BF), second).astype(F32)
    part = (near[0, 0] + far[0, 0] + one[0] + two).astype(BF)
    return jnp.sum(swap_all(part, "z").astype(F32), axis=0)


def on_device(
    tokens,
    image_tokens,
    caption_lengths,
    arrival_order,
    w_qkv,
    w_out,
    w_cross_q,
    w_cross_kv,
    w_cross_out,
    w_up,
    w_down,
    small_params,
    cotangent,
):
    sizes = [lax.axis_size(a) for a in AXES]
    devices = sizes[0] * sizes[1] * sizes[2] * sizes[3]
    height = D // devices
    rows = tokens.shape[0]
    captions = caption_lengths.shape[1]
    slots = captions * CAP_LEN
    images = captions * IMG
    me = jnp.stack([lax.axis_index(a) for a in AXES]).astype(jnp.int32).reshape(1, 4)

    own = jnp.concatenate(
        [
            w_qkv.reshape(height, -1),
            w_out.reshape(height, -1),
            w_cross_q.reshape(height, -1),
            w_cross_kv.reshape(height, -1),
            w_cross_out.reshape(height, -1),
            w_up.reshape(height, D, FOLD).swapaxes(1, 2).reshape(height, FF),
            w_down.reshape(height, FF),
        ],
        axis=1,
    )
    weights = lax.all_gather(own, AXES, axis=0, tiled=True)

    tok = swap_all(tokens, ("y", "c"))
    cot = swap_all(cotangent, ("y", "c"))
    flat = swap_all(
        jnp.broadcast_to(small_params[None, None], (devices, 1, small_params.shape[0])), AXES
    )
    table = flat.reshape(-1, D).astype(F32)
    table = jnp.concatenate(
        [table[:6], table[6 : 6 + FOLD].reshape(D, FOLD).T, table[6 + FOLD :]], axis=0
    )
    img = image_tokens.reshape(images, D)

    slotted, normed_self, grad_slot = run(
        place_kernel,
        [((rows, D), BF)] * 3,
        [VM] * 4,
        [],
        4 * rows * rows * D,
        arrival_order, tok, cot, table,
    )
    sems = lambda n: pltpu.SemaphoreType.DMA((n,))
    vmem = pltpu.VMEM
    (kv,) = run(
        kv_kernel,
        [((images, 2 * D), BF)],
        [VM, HB],
        [vmem((D, 2 * D), BF), sems(1)],
        4 * images * D * D,
        img, weights,
    )
    projected, self_probs, self_mixed, after_self, normed_cross, query_slots = run(
        self_kernel,
        [
            ((rows, 3 * D), BF),
            ((PAIRS, 2 * rows, rows), BF),
            ((rows, D), BF),
            ((rows, D), F32),
            ((rows, D), BF),
            ((slots, D), BF),
        ],
        [SM, VM, VM, VM, HB],
        [vmem((D, 3 * D), BF), vmem((D, D), BF), vmem((D, D), BF), sems(3)],
        10 * rows * D * D,
        caption_lengths, slotted, normed_self, table, weights,
    )
    cross_probs, cross_mixed, after_cross, normed_mlp = run(
        cross_kernel,
        [
            ((captions * PAIRS, 2 * CAP_LEN, IMG), BF),
            ((rows, D), BF),
            ((rows, D), F32),
            ((rows, D), BF),
        ],
        [SM, VM, VM, VM, VM, HB],
        [vmem((D, D), BF), vmem((slots, D), BF), sems(1)],
        10 * rows * D * D,
        caption_lengths, query_slots, kv, after_self, table, weights,
    )
    active, grad_hidden, layer_rows, grad_after, small_mlp = run(
        mlp_kernel,
        [
            ((rows, FF), BF),
            ((rows, FF), BF),
            ((rows, D), BF),
            ((rows, D), F32),
            ((8, D), F32),
        ],
        [VM, VM, VM, VM, VM, HB],
        [vmem((FOLD, D, D), BF), vmem((FOLD, D, D), BF), sems(2 * FOLD)],
        8 * rows * D * FF,
        arrival_order, after_cross, normed_mlp, grad_slot, table, weights,
    )

    def weight_grads(first, pieces, *args):
        shape = (2, 2, sizes[0], height, FF)
        return run(
            functools.partial(weight_grad_kernel, first, pieces),
            [(shape, BF)] * 2,
            [SM] + [VM] * len(args),
            [],
            2 * rows * D * FF,
            me, *args,
        )

    def owned_sum(first, pieces, *args):
        second = "x" if first == "y" else "y"
        if height % 8 == 0 and sizes[1] == 2 and sizes[2] == 2:
            return reduce_unit(*weight_grads(first, pieces, *args), first, second)
        whole = jnp.concatenate(
            [
                t_mm(args[a][:, a0 : a0 + D], args[b][:, b0 : b0 + width])
                for a, a0, b, b0, width, _ in pieces
            ],
            axis=1,
        )
        parts = whole.astype(BF).reshape(devices, height, FF)
        return jnp.sum(swap_all(parts, AXES).astype(F32), axis=0)

    sum_down = owned_sum(
        "y", [(0, j * D, 1, 0, D, j * D) for j in range(FOLD)], active, grad_slot
    )
    sum_up = owned_sum("x", [(0, 0, 1, 0, FF, 0)], normed_mlp, grad_hidden)

    branch_cross, grad_query, grad_kv, grad_state, small_cross = run(
        cross_back_kernel,
        [
            ((rows, D), BF),
            ((rows, D), BF),
            ((images, 2 * D), BF),
            ((rows, D), F32),
            ((8, D), F32),
        ],
        [SM, VM, VM, VM, VM, VM, VM, HB],
        [
            vmem((D, D), BF),
            vmem((D, D), BF),
            vmem((slots, D), BF),
            vmem((slots, D), BF),
            sems(2),
        ],
        14 * rows * D * D,
        caption_lengths, grad_after, cross_probs, query_slots, kv, after_self, table, weights,
    )
    sum_cross = owned_sum(
        "y",
        [(0, 0, 1, 0, D, 0), (2, 0, 3, 0, 2 * D, D), (4, 0, 5, 0, D, 3 * D)],
        normed_cross, grad_query, img, grad_kv, cross_mixed, branch_cross,
    )
    branch_self, grad_projected, token_rows, small_self = run(
        self_back_kernel,
        [
            ((rows, D), BF),
            ((rows, 3 * D), BF),
            ((rows, D), BF),
            ((8, D), F32),
        ],
        [VM, VM, VM, VM, VM, VM, HB],
        [vmem((D, D), BF), vmem((D, 3 * D), BF), vmem((rows, D), BF), sems(2)],
        14 * rows * D * D,
        arrival_order, grad_state, self_probs, projected, slotted, table, weights,
    )
    sum_self = owned_sum(
        "x",
        [(0, 0, 1, 0, 3 * D, 0), (2, 0, 3, 0, D, 3 * D)],
        normed_self, grad_projected, self_mixed, branch_self,
    )
    (grad_image,) = run(
        image_grad_kernel,
        [((images, D), BF)],
        [VM, HB],
        [vmem((D, 2 * D), BF), sems(1)],
        4 * images * D * D,
        grad_kv, weights,
    )

    grad_small = jnp.concatenate(
        [
            small_self[0:1],
            small_cross[0:1],
            small_mlp[0:1],
            small_self[1:2],
            small_cross[1:2],
            small_mlp[1:2],
            small_mlp[2 : 2 + FOLD].T.reshape(FOLD, D),
            small_mlp[6:7],
        ],
        axis=0,
    )
    parts = grad_small.astype(BF).reshape(devices, 1, -1)
    sum_small = jnp.sum(swap_all(parts, AXES).astype(F32), axis=(0, 1))

    layer_out = swap_all(layer_rows, ("y", "c"))
    grad_tokens = swap_all(token_rows, ("y", "c"))
    return (
        layer_out,
        grad_tokens,
        grad_image.reshape(image_tokens.shape),
        sum_self[:, : 3 * D].reshape(-1),
        sum_self[:, 3 * D :].reshape(-1),
        sum_cross[:, :D].reshape(-1),
        sum_cross[:, D : 3 * D].reshape(-1),
        sum_cross[:, 3 * D :].reshape(-1),
        sum_up.reshape(height, FOLD, D).swapaxes(1, 2).reshape(-1),
        sum_down.reshape(-1),
        sum_small,
    )


def solution(mesh):
    dp, fsdp = mesh.shape["dp"], mesh.shape["fsdp"]
    split = Mesh(mesh.devices.reshape(dp // 2, 2, fsdp // 2, 2), AXES)
    rows, flat = P(AXES, None), P(AXES)
    cube = P(AXES, None, None)
    return jax.shard_map(
        on_device,
        mesh=split,
        in_specs=(rows, cube, rows, rows) + (flat,) * 8 + (rows,),
        out_specs=(rows, rows, cube) + (flat,) * 8,
        check_vma=False,
    )
```

time: 1140 us -> 432 us (0.38)
  waiting for transfers between devices: 627 us -> 177 us
  local copies, waits for them, and re-layouts: 187 us -> 53.7 us
  matrix products: 109 us -> 0 us
  Pallas kernels: 0 us -> 63.1 us
  starting transfers between devices: 82.5 us -> 42.6 us
  blocking collectives: 41.9 us -> 14.4 us
    all_to_all x20 -> x9, waiting for transfers between devices: 376 us -> 60.8 us  [swap_all(): return lax.all_to_all(value, axes, split_axis=0, concat_axis=0, tiled=True)]
    all_gather x7 -> x1, waiting for transfers between devices: 246 us -> 92.8 us  [on_device(): weights = lax.all_gather(own, AXES, axis=0, tiled=True)]
    dot_general x33 -> x0, matrix products: 109 us -> none  [the longest x1 11.9 us: forward(): jnp.dot(normed_mlp, mat_up, preferred_element_type=jnp.float32) + up_bias]
    convert_element_type x17 -> x2, local copies, waits for them, and re-layouts: 65.5 us -> 0.22 us  [the longest x1 0.12 us: on_device(): parts = grad_small.astype(BF).reshape(devices, 1, -1)]
    pallas_call x0 -> x12, Pallas kernels: none -> 63.1 us  [run(): pl.pallas_call(kernel, out_shape=shapes, in_specs=specs, out_specs=[VM] *...]
    convert_element_type x3 -> x26, other arithmetic: 3.44 us -> 55.7 us  [the longest x4 12.4 us: reduce_unit(): part = (near[0, 0] + far[0, 0] + one[0] + two).astype(BF)]
    all_to_all x20 -> x9, starting transfers between devices: 82.3 us -> 34.4 us  [swap_all(): return lax.all_to_all(value, axes, split_axis=0, concat_axis=0, tiled=True)]
    unnamed x1 -> x0, blocking collectives: 41.9 us -> none
  transfers between devices with their start and end apart: 27 -> 22, of which waited for: 19 -> 11; matrix products, arithmetic and copies ran while one was open for 24% -> 19% of each run, Pallas kernels for 0% -> 4%
where the time goes in v1:
time: 432 us; the launch traced here: 426 us
  waiting for transfers between devices  177 us (41%)
  Pallas kernels  63.1 us (15%)
  other arithmetic  60.9 us (14%)
  local copies, waits for them, and re-layouts  53.7 us (12%)
  starting transfers between devices  42.6 us (10%)
  between operations  15 us (3%)
  blocking collectives  14.4 us (3%)
    all_gather x1, waiting for transfers between devices, on_device(): weights = lax.all_gather(own, AXES, axis=0, tiled=True)  92.8 us
    pallas_call x12, Pallas kernels, run(): pl.pallas_call(kernel, out_shape=shapes, in_specs=specs, out_specs=[VM] *...  63.1 us
    all_to_all x9, waiting for transfers between devices, swap_all(): return lax.all_to_all(value, axes, split_axis=0, concat_axis=0, tiled=True)  60.8 us
    all_to_all x9, starting transfers between devices, swap_all(): return lax.all_to_all(value, axes, split_axis=0, concat_axis=0, tiled=True)  34.4 us
    ppermute x12, waiting for transfers between devices, flip(): return lax.ppermute(value, axis, [(0, 1), (1, 0)])  23.3 us
    all_to_all x1, blocking collectives, swap_all(): return lax.all_to_all(value, axes, split_axis=0, concat_axis=0, tiled=True)  14.4 us
    unnamed x66, local copies, waits for them, and re-layouts  13.1 us
    convert_element_type x4, other arithmetic, reduce_unit(): part = (near[0, 0] + far[0, 0] + one[0] + two).astype(BF)  12.4 us
  transfers between devices with their start and end apart: 22, of which 11 were waited for; matrix products, arithmetic and copies ran while one was open for 19% of the time, Pallas kernels for 4%

profile of v1, /device:TPU:0, one launch (start us, length us, event | category | flops | bytes accessed | tf_op | source)
XLA Modules:
  0.0 426.4 jit_solution(6168282836233860543)
XLA Ops:
  11.8 11.9 %reshape.134 = bf16[24,768,4]{2,1,0:T(8,128)(2,1)} reshape(bf16[73728]{0:T(1024)(128)(2,1)} %param.22) | data formatting | bytes 294912 | tf_op jit(solution)/shard_map/reshape | solution.py:450
  23.7 4.0 copy.33
  30.2 14.4 %all_to_all.76 = bf16[32,2,132]{2,1,0:T(2,128)(2,1)S(1)} all-to-all(bf16[32,2,132]{2,1,0:T(2,128)(2,1)S(1)} %reshape.151), channel_id=1, replica_groups=mesh['z'=4,'x'=2,'y'=2,'c'=2] {'z','x','y','c'}, dimensions={0} | all-to-all | bytes 33792 | tf_op jit(solution)/shard_map/all_to_all | solution.py:407
  44.5 3.4 all-to-all-start
  48.1 5.6 %all-to-all-done = bf16[4,40,768]{2,1,0:T(8,128)(2,1)S(1)} async-done(((bf16[4,40,768]{2,1,0:T(8,128)(2,1)}), bf16[4,40,768]{2,1,0:T(8,128)(2,1)S(1)}, u32[]{:S(2)}, u32[]{:S(2)}) %all-to-all-start) | async-done | bytes 245792 | tf_op jit(solution)/shard_map/all_to_all | solution.py:407
  53.8 3.6 all-to-all-start.1
  58.2 4.8 %all-to-all-done.1 = bf16[4,40,768]{2,1,0:T(8,128)(2,1)S(1)} async-done(((bf16[4,40,768]{2,1,0:T(8,128)(2,1)}), bf16[4,40,768]{2,1,0:T(8,128)(2,1)S(1)}, u32[]{:S(2)}, u32[]{:S(2)}) %all-to-all-start.1) | async-done | bytes 245792 | tf_op jit(solution)/shard_map/all_to_all | solution.py:407
  63.4 92.8 %all-gather.2.cloned.1.call-done.weights = bf16[768,12288]{1,0:T(8,128)(2,1)} async-done(((bf16[24,12288]{1,0:T(8,128)(2,1)}), bf16[768,12288]{1,0:T(8,128)(2,1)}) %all-gather.2.cloned.1.call-update) | async-done | bytes 18874384 | tf_op jit(solution)/shard_map/all_gather | solution.py:455
  156.3 4.3 %shard_map.214.kv = bf16[1024,1536]{1,0:T(8,128)(2,1)S(1)} custom-call(bf16[1024,768]{1,0:T(8,128)(2,1)S(1)} %bitcast.121, bf16[768,12288]{1,0:T(8,128)(2,1)} %all-gather.2.cloned.1.call-done.weights), custom_call_target="tpu_custom_call" | custom-call | flops 2415919104 | bytes 23592960 | tf_op jit(solution)/shard_map/pallas_call | solution.py:391
  160.6 5.7 %shard_map.213 = (bf16[160,2304]{1,0:T(8,128)(2,1)S(1)}, bf16[6,320,160]{2,1,0:T(8,128)(2,1)S(1)}, bf16[160,768]{1,0:T(8,128)(2,1)S(1)}, f32[160,768]{1,0:T(8,12...) custom-call(s32[1,4]{1,0:T(1,128)S(1)} %copy-done.4, bf16[160,768]{1,0:T(8,128)(2,1)S(1)} %get-tuple-element.46.slotted, ...), custom_call_target="tpu_custom_call" | custom-call | flops 943718400 | bytes 22127632 | tf_op jit(solution)/shard_map/pallas_call | solution.py:391
  166.3 4.5 %shard_map.215 = (bf16[24,128,256]{2,1,0:T(8,128)(2,1)S(1)}, bf16[160,768]{1,0:T(8,128)(2,1)S(1)}, f32[160,768]{1,0:T(8,128)S(1)}, bf16[160,768]{1,0:T(8,128)(2,1)S(1)}) custom-call(s32[1,4]{1,0:T(1,128)S(1)} %copy-done.4, bf16[256,768]{1,0:T(8,128)(2,1)S(1)} %get-tuple-element.48.query_slots, bf16[1024,1536]{1,0:T(8,128)(2,1)S(1)} %shard_map.214.kv, ...), custom_call_target="tpu_custom_call" | custom-call | flops 943718400 | bytes 25494544 | tf_op jit(solution)/shard_map/pallas_call | solution.py:391
  170.8 9.0 %shard_map.216 = (bf16[160,3072]{1,0:T(8,128)(2,1)S(1)}, bf16[160,3072]{1,0:T(8,128)(2,1)S(1)}, bf16[160,768]{1,0:T(8,128)(2,1)}, f32[160,768]{1,0:T(8,128)S(1)}, f32[8,768]{1,0:T(8,128)S(1)}) custom-call(s32[1,160]{1,0:T(1,128)S(1)} %copy-done.3, f32[160,768]{1,0:T(8,128)S(1)} %get-tuple-element.50.after_cross, ...), custom_call_target="tpu_custom_call" | custom-call | flops 3019898880 | bytes 22619776 | tf_op jit(solution)/shard_map/pallas_call | solution.py:391
  179.8 10.8 %shard_map.217 = (bf16[160,768]{1,0:T(8,128)(2,1)S(1)}, bf16[160,768]{1,0:T(8,128)(2,1)S(1)}, bf16[1024,1536]{1,0:T(8,128)(2,1)S(1)}, f32[160,768]{1,0:T(8,128)S(1)}, f32[8,768]{1,0:T(8,128)S(1)}) custom-call(s32[1,4]{1,0:T(1,128)S(1)} %copy-done.4, f32[160,768]{1,0:T(8,128)S(1)} %get-tuple-element.54.grad_after, ...), custom_call_target="tpu_custom_call" | custom-call | flops 1321205760 | bytes 29156368 | tf_op jit(solution)/shard_map/pallas_call | solution.py:391
  192.2 7.0 %shard_map.218 = (bf16[160,768]{1,0:T(8,128)(2,1)S(1)}, bf16[160,2304]{1,0:T(8,128)(2,1)S(1)}, bf16[160,768]{1,0:T(8,128)(2,1)}, f32[8,768]{1,0:T(8,128)S(1)}) custom-call(s32[1,160]{1,0:T(1,128)S(1)} %copy-done.3, f32[160,768]{1,0:T(8,128)S(1)} %get-tuple-element.56.grad_state, bf16[6,320,160]{2,1,0:T(8,128)(2,1)S(1)} %get-tuple-element.57.probs, ...), custom_call_target="tpu_custom_call" | custom-call | flops 1321205760 | bytes 22251136 | tf_op jit(solution)/shard_map/pallas_call | solution.py:391
  199.3 3.4 shard_map.220
  203.0 7.0 %shard_map.221 = (bf16[2,2,4,24,3072]{4,3,2,1,0:T(8,128)(2,1)S(1)}, bf16[2,2,4,24,3072]{4,3,2,1,0:T(8,128)(2,1)}) custom-call(s32[1,4]{1,0:T(1,128)S(1)} %add_bitcast_fusion.me, bf16[160,768]{1,0:T(8,128)(2,1)S(1)} %get-tuple-element.66.refs_0_, bf16[160,768]{1,0:T(8,128)(2,1)S(1)} %get-tuple-element.67.refs_1_, bf16[1024,768]{1,0:T(8,128)(2,1)S(1)} %bitcast.122, ...), custom_call_target="tpu_custom_call" | custom-call | flops 754974720 | bytes 10420240 | tf_op jit(solution)/shard_map/pallas_call | solution.py:391
  210.2 2.8 convert_element_type.130
  213.0 2.7 convert_element_type.139
  218.0 2.7 convert_element_type.148
  220.8 3.5 shard_map.223
  224.5 2.7 convert_element_type.157
  229.5 3.3 all-to-all-start.9
  235.3 3.7 fusion.4
  257.3 10.5 %collective-permute-done.1 = bf16[2,4,24,3072]{3,2,1,0:T(8,128)(2,1)S(1)} collective-permute-done((bf16[2,4,24,3072]{3,2,1,0:T(8,128)(2,1)S(1)}, bf16[2,4,24,3072]{3,2,1,0:T(8,128)(2,1)S(1)}, u32[]{:S(2)}, u32[]{:S(2)}) %collective-permute-start.1) | collective-permute-done | bytes 1179680 | tf_op jit(solution)/shard_map/ppermute | solution.py:403
  268.1 3.2 fusion.30
  274.2 4.0 all-to-all-start.3
  278.3 2.7 fusion.23
  281.4 11.7 %collective-permute-done.7 = bf16[2,4,24,3072]{3,2,1,0:T(8,128)(2,1)S(1)} collective-permute-done((bf16[2,4,24,3072]{3,2,1,0:T(8,128)(2,1)}, bf16[2,4,24,3072]{3,2,1,0:T(8,128)(2,1)S(1)}, u32[]{:S(2)}, u32[]{:S(2)}) %collective-permute-start.7) | collective-permute-done | bytes 1179680 | tf_op jit(solution)/shard_map/ppermute | solution.py:403
  293.4 20.1 %all-to-all-done.3 = bf16[4,40,768]{2,1,0:T(8,128)(2,1)} async-done(((bf16[4,40,768]{2,1,0:T(8,128)(2,1)}), bf16[4,40,768]{2,1,0:T(8,128)(2,1)}, u32[]{:S(2)}, u32[]{:S(2)}) %all-to-all-start.3) | async-done | bytes 245792 | tf_op jit(solution)/shard_map/all_to_all | solution.py:407
  313.5 3.4 all-to-all-start.4
  316.9 3.2 fusion.34
  320.1 2.6 all-to-all-done.4
  323.4 4.9 %all-to-all-start.5 = ((bf16[4,24,3072]{2,1,0:T(8,128)(2,1)}), bf16[4,24,3072]{2,1,0:T(8,128)(2,1)S(1)}, u32[]{:S(2)}, u32[]{:S(2)}) async-start(bf16[4,24,3072]{2,1,0:T(8,128)(2,1)} %fusion.34), calls=%async_computation.5 | async-start | bytes 1179648 | tf_op jit(solution)/shard_map/all_to_all | solution.py:407
  328.3 2.6 fusion.16
  331.3 3.1 convert_element_type.161
  334.4 2.9 fusion.27
  337.3 6.7 %all-to-all-done.5 = bf16[4,24,3072]{2,1,0:T(8,128)(2,1)S(1)} async-done(((bf16[4,24,3072]{2,1,0:T(8,128)(2,1)}), bf16[4,24,3072]{2,1,0:T(8,128)(2,1)S(1)}, u32[]{:S(2)}, u32[]{:S(2)}) %all-to-all-start.5) | async-done | bytes 589856 | tf_op jit(solution)/shard_map/all_to_all | solution.py:407
  344.0 3.5 all-to-all-start.6
  347.5 3.0 fusion.9
  351.1 2.8 fusion.20
  353.9 8.9 %all-to-all-done.6 = bf16[4,24,3072]{2,1,0:T(8,128)(2,1)S(1)} async-done(((bf16[4,24,3072]{2,1,0:T(8,128)(2,1)}), bf16[4,24,3072]{2,1,0:T(8,128)(2,1)S(1)}, u32[]{:S(2)}, u32[]{:S(2)}) %all-to-all-start.6) | async-done | bytes 589856 | tf_op jit(solution)/shard_map/all_to_all | solution.py:407
  363.6 4.2 all-to-all-start.7
  367.8 3.4 fusion.13
  371.3 12.0 %all-to-all-done.7 = bf16[4,24,3072]{2,1,0:T(8,128)(2,1)} async-done(((bf16[4,24,3072]{2,1,0:T(8,128)(2,1)}), bf16[4,24,3072]{2,1,0:T(8,128)(2,1)}, u32[]{:S(2)}, u32[]{:S(2)}) %all-to-all-start.7) | async-done | bytes 589856 | tf_op jit(solution)/shard_map/all_to_all | solution.py:407
  383.3 4.2 all-to-all-start.8
  387.4 5.4 %shard_map.219 = bf16[1024,768]{1,0:T(8,128)(2,1)} custom-call(bf16[1024,1536]{1,0:T(8,128)(2,1)S(1)} %copy-done.1, bf16[768,12288]{1,0:T(8,128)(2,1)} %all-gather.2.cloned.1.call-done.weights), custom_call_target="tpu_custom_call" | custom-call | flops 2415919104 | bytes 23592960 | tf_op jit(solution)/shard_map/pallas_call | solution.py:391
  400.4 5.1 %copy.34 = f32[24,768,4]{2,1,0:T(8,128)} copy(f32[24,768,4]{1,2,0:T(4,128)S(1)} %bitcast.133) | data formatting | bytes 589824 | tf_op jit(solution)/shard_map/transpose | solution.py:638
  405.5 9.6 %reshape.146 = f32[73728]{0:T(1024)} reshape(f32[24,768,4]{2,1,0:T(8,128)} %copy.34) | data formatting | bytes 589824 | tf_op jit(solution)/shard_map/reshape | solution.py:638
  (152 shorter events, 54.1 us)
Async XLA Ops:
  7.2 149.1 %all-gather.2.cloned.1.call-start = ((), (), s32[]{:S(2)}) async-start(), calls=%async_computation.10 | async-start | bytes 19464192 | tf_op jit(solution)/shard_map/all_gather | solution.py:455
  23.7 4.0 copy-start.18
  23.7 5.1 %copy-start.19 = (bf16[264]{0:T(512)(128)(2,1)S(1)}, bf16[264]{0:T(512)(128)(2,1)}, u32[]{:S(2)}) copy-start(bf16[264]{0:T(512)(128)(2,1)} %param.24) | copy-start | bytes 1588
  27.7 35.3 %copy-start.3 = (s32[1,160]{1,0:T(1,128)S(1)}, s32[1,160]{1,0:T(1,128)}, u32[]{:S(2)}) copy-start(s32[1,160]{1,0:T(1,128)} %arr.5) | copy-start | bytes 1924
  27.8 128.5 %copy-start.2 = (bf16[4,256,768]{2,1,0:T(8,128)(2,1)S(1)}, bf16[4,256,768]{2,1,0:T(8,128)(2,1)}, u32[]{:S(2)}) copy-start(bf16[4,256,768]{2,1,0:T(8,128)(2,1)} %param.14) | copy-start | bytes 4718596
  27.9 0.8 copy-start.17
  44.5 9.2 %all-to-all-start = ((bf16[4,40,768]{2,1,0:T(8,128)(2,1)}), bf16[4,40,768]{2,1,0:T(8,128)(2,1)S(1)}, u32[]{:S(2)}, u32[]{:S(2)}) async-start(bf16[4,40,768]{2,1,0:T(8,128)(2,1)} %bitcast), calls=%async_computation | async-start | bytes 491520 | tf_op jit(solution)/shard_map/all_to_all | solution.py:407
  53.8 9.2 %all-to-all-start.1 = ((bf16[4,40,768]{2,1,0:T(8,128)(2,1)}), bf16[4,40,768]{2,1,0:T(8,128)(2,1)S(1)}, u32[]{:S(2)}, u32[]{:S(2)}) async-start(bf16[4,40,768]{2,1,0:T(8,128)(2,1)} %bitcast.2), calls=%async_computation.1 | async-start | bytes 491520 | tf_op jit(solution)/shard_map/all_to_all | solution.py:407
  156.3 4.3 %copy-start.4 = (s32[1,4]{1,0:T(1,128)S(1)}, s32[1,4]{1,0:T(1,128)}, u32[]{:S(2)}) copy-start(s32[1,4]{1,0:T(1,128)} %lens.5) | copy-start | bytes 52
  190.6 1.7 copy-start
  202.7 30.1 %collective-permute-start = (bf16[2,2,4,24,3072]{4,3,2,1,0:T(8,128)(2,1)}, bf16[2,2,4,24,3072]{4,3,2,1,0:T(8,128)(2,1)}, u32[]{:S(2)}, u32[]{:S(2)}) collective-permute-start(bf16[2,2,4,24,3072]{4,3,2,1,0:T(8,128)(2,1)} %get-tuple-element.65), channel_id=1, source_target_pairs={{0,1},{1,0},{2,3},{3,2},{4,5},{5,4},{6,7},{7,6},{8,9},{9,8},{10,11... | collective-permute-start | bytes 7077896 | tf_op jit(solution)/shard_map/ppermute | solution.py:403
  210.0 30.6 %collective-permute-start.3 = (bf16[2,2,4,24,3072]{4,3,2,1,0:T(8,128)(2,1)}, bf16[2,2,4,24,3072]{4,3,2,1,0:T(8,128)(2,1)}, u32[]{:S(2)}, u32[]{:S(2)}) collective-permute-start(bf16[2,2,4,24,3072]{4,3,2,1,0:T(8,128)(2,1)} %get-tuple-element.71), channel_id=1, source_target_pairs={{0,1},{1,0},{2,3},{3,2},{4,5},{5,4},{6,7},{7,6},{8,9},{9,8},{10,11... | collective-permute-start | bytes 7077896 | tf_op jit(solution)/shard_map/ppermute | solution.py:403
  217.7 28.9 %collective-permute-start.6 = (bf16[2,2,4,24,3072]{4,3,2,1,0:T(8,128)(2,1)S(1)}, bf16[2,2,4,24,3072]{4,3,2,1,0:T(8,128)(2,1)}, u32[]{:S(2)}, u32[]{:S(2)}) collective-permute-start(bf16[2,2,4,24,3072]{4,3,2,1,0:T(8,128)(2,1)S(1)} %get-tuple-element.74), channel_id=1, source_target_pairs={{0,1},{1,0},{2,3},{3,2},{4,5},{5,4},{6,7},{7,6},{8,9},{9,8},{10,11... | collective-permute-start | bytes 7077896 | tf_op jit(solution)/shard_map/ppermute | solution.py:403
  224.2 27.8 %collective-permute-start.9 = (bf16[2,2,4,24,3072]{4,3,2,1,0:T(8,128)(2,1)}, bf16[2,2,4,24,3072]{4,3,2,1,0:T(8,128)(2,1)}, u32[]{:S(2)}, u32[]{:S(2)}) collective-permute-start(bf16[2,2,4,24,3072]{4,3,2,1,0:T(8,128)(2,1)} %get-tuple-element.77), channel_id=1, source_target_pairs={{0,1},{1,0},{2,3},{3,2},{4,5},{5,4},{6,7},{7,6},{8,9},{9,8},{10,11... | collective-permute-start | bytes 7077896 | tf_op jit(solution)/shard_map/ppermute | solution.py:403
  229.5 44.7 %all-to-all-start.9 = ((bf16[32,2,132]{2,1,0:T(2,128)(2,1)}), bf16[32,2,132]{2,1,0:T(2,128)(2,1)}, u32[]{:S(2)}, u32[]{:S(2)}) async-start(bf16[32,2,132]{2,1,0:T(2,128)(2,1)} %reshape.153), calls=%async_computation.9 | async-start | bytes 65536 | tf_op jit(solution)/shard_map/all_to_all | solution.py:407
  232.8 10.1 %slice-start.4 = ((s8[4718592]{0:T(1024)(128)(4,1)}), s8[4194304]{0:T(1024)(128)(4,1)S(1)}, s32[]{:S(2)}) async-start(s8[4718592]{0:T(1024)(128)(4,1)} %bitcast.130), calls=%async_computation.15 | async-start | bytes 8388608
  235.2 32.9 %copy-start.8 = (f32[2,2,4,24,3072]{4,3,2,1,0:T(8,128)}, f32[2,2,4,24,3072]{4,3,2,1,0:T(8,128)S(1)}, u32[]{:S(2)}) copy-start(f32[2,2,4,24,3072]{4,3,2,1,0:T(8,128)S(1)} %convert_element_type.131) | copy-start | bytes 14155780
  235.2 7.7 %slice-start.5 = ((s8[4718592]{0:T(1024)(128)(4,1)}), s8[524288]{0:T(1024)(128)(4,1)S(1)}, s32[]{:S(2)}) async-start(s8[4718592]{0:T(1024)(128)(4,1)} %bitcast.130), calls=%async_computation.16 | async-start | bytes 1048576
  238.9 28.9 %collective-permute-start.1 = (bf16[2,4,24,3072]{3,2,1,0:T(8,128)(2,1)S(1)}, bf16[2,4,24,3072]{3,2,1,0:T(8,128)(2,1)S(1)}, u32[]{:S(2)}, u32[]{:S(2)}) collective-permute-start(bf16[2,4,24,3072]{3,2,1,0:T(8,128)(2,1)S(1)} %fusion.4), channel_id=1, source_target_pairs={{0,4},{4,0},{1,5},{5,1},{2,6},{6,2},{3,7},{7,3},{8,12},{12,8},{9,1... | collective-permute-start | bytes 3538952 | tf_op jit(solution)/shard_map/ppermute | solution.py:403
  240.6 8.4 %slice-start.2 = ((s8[4718592]{0:T(1024)(128)(4,1)}), s8[4194304]{0:T(1024)(128)(4,1)S(1)}, s32[]{:S(2)}) async-start(s8[4718592]{0:T(1024)(128)(4,1)} %bitcast.128), calls=%async_computation.13 | async-start | bytes 8388608
  243.0 2.1 copy-start.7
  243.0 6.0 %slice-start.3 = ((s8[4718592]{0:T(1024)(128)(4,1)}), s8[524288]{0:T(1024)(128)(4,1)S(1)}, s32[]{:S(2)}) async-start(s8[4718592]{0:T(1024)(128)(4,1)} %bitcast.128), calls=%async_computation.14 | async-start | bytes 1048576
  245.1 28.9 %collective-permute-start.4 = (bf16[2,4,24,3072]{3,2,1,0:T(8,128)(2,1)S(1)}, bf16[2,4,24,3072]{3,2,1,0:T(8,128)(2,1)S(1)}, u32[]{:S(2)}, u32[]{:S(2)}) collective-permute-start(bf16[2,4,24,3072]{3,2,1,0:T(8,128)(2,1)S(1)} %fusion.5), channel_id=1, source_target_pairs={{0,2},{2,0},{1,3},{3,1},{4,6},{6,4},{5,7},{7,5},{8,10},{10,8},{9,1... | collective-permute-start | bytes 3538952 | tf_op jit(solution)/shard_map/ppermute | solution.py:403
  246.6 7.7 %slice-start = ((s8[4718592]{0:T(1024)(128)(4,1)}), s8[4194304]{0:T(1024)(128)(4,1)S(1)}, s32[]{:S(2)}) async-start(s8[4718592]{0:T(1024)(128)(4,1)} %bitcast.126), calls=%async_computation.11 | async-start | bytes 8388608
  249.0 2.5 copy-start.6
  249.0 5.3 %slice-start.1 = ((s8[4718592]{0:T(1024)(128)(4,1)}), s8[524288]{0:T(1024)(128)(4,1)S(1)}, s32[]{:S(2)}) async-start(s8[4718592]{0:T(1024)(128)(4,1)} %bitcast.126), calls=%async_computation.12 | async-start | bytes 1048576
  251.5 41.6 %collective-permute-start.7 = (bf16[2,4,24,3072]{3,2,1,0:T(8,128)(2,1)}, bf16[2,4,24,3072]{3,2,1,0:T(8,128)(2,1)S(1)}, u32[]{:S(2)}, u32[]{:S(2)}) collective-permute-start(bf16[2,4,24,3072]{3,2,1,0:T(8,128)(2,1)} %fusion.6), channel_id=1, source_target_pairs={{0,4},{4,0},{1,5},{5,1},{2,6},{6,2},{3,7},{7,3},{8,12},{12,8},{9,1... | collective-permute-start | bytes 3538952 | tf_op jit(solution)/shard_map/ppermute | solution.py:403
  254.3 2.6 copy-start.5
  256.9 74.4 %collective-permute-start.10 = (bf16[2,4,24,3072]{3,2,1,0:T(8,128)(2,1)}, bf16[2,4,24,3072]{3,2,1,0:T(8,128)(2,1)}, u32[]{:S(2)}, u32[]{:S(2)}) collective-permute-start(bf16[2,4,24,3072]{3,2,1,0:T(8,128)(2,1)} %fusion.7), channel_id=1, source_target_pairs={{0,2},{2,0},{1,3},{3,1},{4,6},{6,4},{5,7},{7,5},{8,10},{10,8},{9,1... | collective-permute-start | bytes 3538952 | tf_op jit(solution)/shard_map/ppermute | solution.py:403
  268.1 4.8 %copy-start.11 = (f32[2,4,24,3072]{3,2,1,0:T(8,128)}, f32[2,4,24,3072]{3,2,1,0:T(8,128)S(1)}, u32[]{:S(2)}) copy-start(f32[2,4,24,3072]{3,2,1,0:T(8,128)S(1)} %convert_element_type.134) | copy-start | bytes 7077892
  271.3 45.6 %collective-permute-start.2 = (bf16[4,24,3072]{2,1,0:T(8,128)(2,1)}, bf16[4,24,3072]{2,1,0:T(8,128)(2,1)}, u32[]{:S(2)}, u32[]{:S(2)}) collective-permute-start(bf16[4,24,3072]{2,1,0:T(8,128)(2,1)} %fusion.30), channel_id=1, source_target_pairs={{0,2},{2,0},{1,3},{3,1},{4,6},{6,4},{5,7},{7,5},{8,10},{10,8},{9,1... | collective-permute-start | bytes 1769480 | tf_op jit(solution)/shard_map/ppermute | solution.py:403
  274.2 7.2 %copy-start.9 = (f32[2,4,24,3072]{3,2,1,0:T(8,128)}, f32[2,4,24,3072]{3,2,1,0:T(8,128)S(1)}, u32[]{:S(2)}) copy-start(f32[2,4,24,3072]{3,2,1,0:T(8,128)S(1)} %convert_element_type.143) | copy-start | bytes 7077892
  274.2 39.3 %all-to-all-start.3 = ((bf16[4,40,768]{2,1,0:T(8,128)(2,1)}), bf16[4,40,768]{2,1,0:T(8,128)(2,1)}, u32[]{:S(2)}, u32[]{:S(2)}) async-start(bf16[4,40,768]{2,1,0:T(8,128)(2,1)} %bitcast.7), calls=%async_computation.3 | async-start | bytes 491520 | tf_op jit(solution)/shard_map/all_to_all | solution.py:407
  280.9 53.5 %collective-permute-start.5 = (bf16[4,24,3072]{2,1,0:T(8,128)(2,1)}, bf16[4,24,3072]{2,1,0:T(8,128)(2,1)}, u32[]{:S(2)}, u32[]{:S(2)}) collective-permute-start(bf16[4,24,3072]{2,1,0:T(8,128)(2,1)} %fusion.23), channel_id=1, source_target_pairs={{0,4},{4,0},{1,5},{5,1},{2,6},{6,2},{3,7},{7,3},{8,12},{12,8},{9,1... | collective-permute-start | bytes 1769480 | tf_op jit(solution)/shard_map/ppermute | solution.py:403
  313.5 9.2 %all-to-all-start.4 = ((bf16[4,40,768]{2,1,0:T(8,128)(2,1)}), bf16[4,40,768]{2,1,0:T(8,128)(2,1)S(1)}, u32[]{:S(2)}, u32[]{:S(2)}) async-start(bf16[4,40,768]{2,1,0:T(8,128)(2,1)} %bitcast.9), calls=%async_computation.4 | async-start | bytes 491520 | tf_op jit(solution)/shard_map/all_to_all | solution.py:407
  322.7 0.7 copy-start.15
  323.4 20.6 %all-to-all-start.5 = ((bf16[4,24,3072]{2,1,0:T(8,128)(2,1)}), bf16[4,24,3072]{2,1,0:T(8,128)(2,1)S(1)}, u32[]{:S(2)}, u32[]{:S(2)}) async-start(bf16[4,24,3072]{2,1,0:T(8,128)(2,1)} %fusion.34), calls=%async_computation.5 | async-start | bytes 1179648 | tf_op jit(solution)/shard_map/all_to_all | solution.py:407
  330.9 3.4 copy-start.10
  330.9 20.1 %collective-permute-start.8 = (bf16[4,24,3072]{2,1,0:T(8,128)(2,1)}, bf16[4,24,3072]{2,1,0:T(8,128)(2,1)}, u32[]{:S(2)}, u32[]{:S(2)}) collective-permute-start(bf16[4,24,3072]{2,1,0:T(8,128)(2,1)} %fusion.16), channel_id=1, source_target_pairs={{0,2},{2,0},{1,3},{3,1},{4,6},{6,4},{5,7},{7,5},{8,10},{10,8},{9,1... | collective-permute-start | bytes 1769480 | tf_op jit(solution)/shard_map/ppermute | solution.py:403
  344.0 6.5 %copy-start.12 = (bf16[4,24,3072]{2,1,0:T(8,128)(2,1)}, bf16[4,24,3072]{2,1,0:T(8,128)(2,1)S(1)}, u32[]{:S(2)}) copy-start(bf16[4,24,3072]{2,1,0:T(8,128)(2,1)S(1)} %all-to-all-done.5) | copy-start | bytes 1769476
  344.0 18.8 %all-to-all-start.6 = ((bf16[4,24,3072]{2,1,0:T(8,128)(2,1)}), bf16[4,24,3072]{2,1,0:T(8,128)(2,1)S(1)}, u32[]{:S(2)}, u32[]{:S(2)}) async-start(bf16[4,24,3072]{2,1,0:T(8,128)(2,1)} %fusion.27), calls=%async_computation.6 | async-start | bytes 1179648 | tf_op jit(solution)/shard_map/all_to_all | solution.py:407
  350.5 17.3 %collective-permute-start.11 = (bf16[4,24,3072]{2,1,0:T(8,128)(2,1)}, bf16[4,24,3072]{2,1,0:T(8,128)(2,1)}, u32[]{:S(2)}, u32[]{:S(2)}) collective-permute-start(bf16[4,24,3072]{2,1,0:T(8,128)(2,1)} %fusion.9), channel_id=1, source_target_pairs={{0,4},{4,0},{1,5},{5,1},{2,6},{6,2},{3,7},{7,3},{8,12},{12,8},{9,1... | collective-permute-start | bytes 1769480 | tf_op jit(solution)/shard_map/ppermute | solution.py:403
  362.8 0.8 copy-start.13
  363.6 19.6 %all-to-all-start.7 = ((bf16[4,24,3072]{2,1,0:T(8,128)(2,1)}), bf16[4,24,3072]{2,1,0:T(8,128)(2,1)}, u32[]{:S(2)}, u32[]{:S(2)}) async-start(bf16[4,24,3072]{2,1,0:T(8,128)(2,1)} %fusion.20), calls=%async_computation.7 | async-start | bytes 1179648 | tf_op jit(solution)/shard_map/all_to_all | solution.py:407
  367.8 19.6 %copy-start.1 = (bf16[1024,1536]{1,0:T(8,128)(2,1)S(1)}, bf16[1024,1536]{1,0:T(8,128)(2,1)}, u32[]{:S(2)}) copy-start(bf16[1024,1536]{1,0:T(8,128)(2,1)} %copy-done) | copy-start | bytes 9437188
  383.3 31.9 %all-to-all-start.8 = ((bf16[4,24,3072]{2,1,0:T(8,128)(2,1)}), bf16[4,24,3072]{2,1,0:T(8,128)(2,1)}, u32[]{:S(2)}, u32[]{:S(2)}) async-start(bf16[4,24,3072]{2,1,0:T(8,128)(2,1)} %fusion.13), calls=%async_computation.8 | async-start | bytes 1179648 | tf_op jit(solution)/shard_map/all_to_all | solution.py:407
  392.9 4.1 copy-start.14
  405.5 13.2 %copy-start.16 = (bf16[4,40,768]{2,1,0:T(8,128)(2,1)S(1)}, bf16[4,40,768]{2,1,0:T(8,128)(2,1)}, u32[]{:S(2)}) copy-start(bf16[4,40,768]{2,1,0:T(8,128)(2,1)} %copy-done.15) | copy-start | bytes 737284
Sparse Core Ops, SparseCore 0:
  28.8 127.3 all-gather.1
